TPU v7x, 512 devices: a whole 4x8x8 slice. The times are simulated.
512 devices in a mesh: patch: 16 (over z, core), epoch: 8 (over y_hi, x), band: 4 (over y_lo).
Axes of the slice: x: 4, y: 8 (y_hi: 2, y_lo: 4; y = y_hi * 4 + y_lo), z: 8, core: 2. Of those that a mesh axis runs over, the one named last changes fastest.
Arguments:
- exposures: bfloat16 [64, 2048, 2048], P(('band', 'epoch'), 'patch'), parts along dimension 0, may hold values from -6 to 6
- inv_variance: bfloat16 [64, 2048, 2048], P(('band', 'epoch'), 'patch'), parts along dimension 0, may hold values from 0.25 to 4
- strip_bounds: int32 [64, 2], P(('band', 'epoch')), parts along dimension 0, may hold values from 0 to 16, as said below
- kernel_index: int32 [64, 2, 2], P(('band', 'epoch')), parts along dimension 0, may hold values from 0 to 15
- basis_bank: float32 [16, 21], replicated, may hold values from 0.05 to 1
Outputs:
- coadd: float32 [8192, 2048], P(('band', 'patch'), 'epoch'), parts along dimension 0
- depth_map: float32 [8192, 2048], P(('band', 'patch'), 'epoch'), parts along dimension 0
There are 4 independent parts, one for each index of `band`. A program takes and returns all parts, laid end to end along the dimension named above; an argument that names none is the same for every part. Nothing has to cross between parts.
Inputs may be any that keep to these rules, and one draw needn't show every extreme that they name: `strip_bounds`: each row is a pair lower < upper of strip units; exposure 0 covers the whole window.
All inputs are finite; a program needn't handle non-finite values.
Results may differ from a plain program's by a relative error of at most 0.0043.
Values may be sent and summed in bfloat16 or wider, within the bound.
No kernel may reach another device: no remote copies, remote signals or barrier semaphores. Data moves between devices by JAX's collectives and lax.ppermute only.
A program may use at most 64 MiB of HBM per device.

v0:
```python
import jax
import jax.numpy as jnp
from jax import lax
from jax.sharding import PartitionSpec as P

UNIT = 128
BLOCK = 256
HALF = 10
NCOMP = 2


def with_halo(array, sides, width):
    for axis, dim in sides:
        devices, length = (lax.axis_size(axis), array.shape[dim])
        up = [(i, (i + 1) % devices) for i in range(devices - 1)]
        down = [(j, i) for i, j in up]
        last = lax.slice_in_dim(array, length - width, length, axis=dim)
        initial = lax.slice_in_dim(array, 0, width, axis=dim)
        before = lax.ppermute(last, axis, up)
        after = lax.ppermute(initial, axis, down)
        array = jnp.concatenate([before, array, after], axis=dim)
    return array


def band_matrix(offsets, taps_row):
    picks = offsets[..., None] == jnp.arange(taps_row.shape[0])
    return jnp.sum(jnp.where(picks, taps_row.astype(jnp.float32), 0.0), axis=-1).astype(
        jnp.bfloat16
    )


def horizontal(pixels, taps_row):
    row_count, width = pixels.shape
    blocks = width // BLOCK
    padded = jnp.pad(pixels, ((0, 0), (BLOCK, BLOCK))).reshape(row_count, blocks + 2, BLOCK)
    window = jnp.concatenate([padded[:, :-2], padded[:, 1:-1], padded[:, 2:]], axis=-1)
    inner = jnp.arange(3 * BLOCK)[:, None]
    outer = jnp.arange(BLOCK)[None, :]
    matrix = band_matrix(inner - BLOCK - outer + HALF, taps_row)
    filtered = jnp.einsum("rbi,ij->rbj", window, matrix, preferred_element_type=jnp.float32)
    return filtered.reshape(row_count, width).astype(jnp.bfloat16)


def vertical(extended, taps_row, row_count):
    target = jnp.arange(row_count)[:, None]
    source = jnp.arange(row_count + 2 * HALF)[None, :]
    matrix = band_matrix(source - target, taps_row)
    return jnp.dot(matrix, extended, preferred_element_type=jnp.float32)


def select_taps(basis_bank, kernel_index):
    picks = (kernel_index[..., None] == jnp.arange(basis_bank.shape[0])).astype(jnp.float32)
    chosen = jnp.einsum("ecsn,nk->ecsk", picks, basis_bank, precision=lax.Precision.HIGHEST)
    normed = chosen / jnp.sum(chosen, axis=-1, keepdims=True)
    factors = jnp.array([1.0, 1.0 / NCOMP], jnp.float32)
    return (normed * factors[None, None, :, None]).astype(jnp.bfloat16)


def shards(exposures, inv_variance, strip_bounds, kernel_index, basis_bank):
    exp_count, row_count, width = exposures.shape
    row_ids = lax.axis_index("patch") * row_count + jnp.arange(row_count, dtype=jnp.int32)
    lower_row = strip_bounds[:, 0:1] * UNIT
    upper_row = strip_bounds[:, 1:2] * UNIT
    covered = (row_ids[None, :] >= lower_row) & (row_ids[None, :] < upper_row)
    masked = jnp.where(covered[:, :, None], exposures, jnp.zeros((), jnp.bfloat16))
    weights = jnp.where(covered[:, :, None], inv_variance.astype(jnp.float32), 0.0)
    taps_all = select_taps(basis_bank, kernel_index)
    empty = jnp.zeros((row_count, width), jnp.float32)
    extended = with_halo(masked, (("patch", 1),), HALF)
    numer = empty
    for index in range(exp_count):
        total = empty
        for comp in range(NCOMP):
            across = horizontal(extended[index], taps_all[index, comp, 0])
            total = total + vertical(across, taps_all[index, comp, 1], row_count)
        numer = numer + weights[index] * total
    denom = jnp.sum(weights, axis=0)
    numer_full, denom_full = lax.psum((numer, denom), "epoch")
    share = width // lax.axis_size("epoch")
    start = lax.axis_index("epoch") * share
    numer_part = lax.dynamic_slice_in_dim(numer_full, start, share, 1)
    denom_part = lax.dynamic_slice_in_dim(denom_full, start, share, 1)
    coadd = numer_part / jnp.maximum(denom_part, 1.0)
    return (coadd, denom_part)


def solution(mesh):
    return jax.shard_map(
        shards,
        mesh=mesh,
        in_specs=(
            P(("band", "epoch"), "patch", None),
            P(("band", "epoch"), "patch", None),
            P(("band", "epoch"), None),
            P(("band", "epoch"), None, None),
            P(),
        ),
        out_specs=(P(("band", "patch"), "epoch"), P(("band", "patch"), "epoch")),
        check_vma=False,
    )
```

profile of v0, /device:TPU:1, one launch (start us, length us, event | category | flops | bytes accessed | tf_op | source)
XLA Modules:
  0.0 194.7 jit_solution(3836411330742269768)
XLA Ops:
  7.3 1.0 multiply_reduce_fusion.1
  8.3 1.5 broadcast_select_fusion
  9.8 5.4 %collective-permute-start = (bf16[2,10,2048]{2,1,0:T(8,128)(2,1)S(1)}, bf16[2,10,2048]{2,1,0:T(8,128)(2,1)S(1)}, u32[]{:S(2)}, u32[]{:S(2)}) collective-permute-start(bf16[2,10,2048]{2,1,0:T(8,128)(2,1)S(1)} %get-tuple-element.26), channel_id=1, source_target_pairs={{0,32},{32,64},{64,96},{96,128},{128,160},{160,192},{192,224},{224... | collective-permute-start | bytes 245768 | tf_op jit(solution)/shard_map/ppermute | solution.py:19
  15.2 4.7 %collective-permute-start.1 = (bf16[2,10,2048]{2,1,0:T(8,128)(2,1)S(1)}, bf16[2,10,2048]{2,1,0:T(8,128)(2,1)S(1)}, u32[]{:S(2)}, u32[]{:S(2)}) collective-permute-start(bf16[2,10,2048]{2,1,0:T(8,128)(2,1)S(1)} %get-tuple-element.27), channel_id=1, source_target_pairs={{32,0},{64,32},{96,64},{128,96},{160,128},{192,160},{224,192},{256... | collective-permute-start | bytes 245768 | tf_op jit(solution)/shard_map/ppermute | solution.py:20
  20.5 1.3 convert_select_fusion
  21.7 7.1 %select_reduce_fusion = (bf16[768,256]{1,0:T(8,128)(2,1)}, bf16[768,256]{1,0:T(8,128)(2,1)}, bf16[768,256]{1,0:T(8,128)(2,1)}, bf16[768,256]{1,0:T(8,128)(2,1)}) fusion(f32[21]{0:T(128)S(1)} %get-tuple-element.29, s32[768,256]{1,0:T(8,128)S(1)} %subtract_add_fusion, f32[21]{0:T(128)S(1)} %get-tuple-element.31, f32[21]{0:T(128)S(1)} %get-tuple-element.33, ...), kind=kLoop, calls=%fused_computation.1 | loop fusion | flops 36372480 | bytes 2359632 | tf_op jit(solution)/shard_map/reduce_sum | solution.py:27
  28.9 0.9 select_reduce_fusion.4
  30.1 0.9 slice_bitcast_fusion.2
  31.1 0.9 pad.10
  32.0 1.5 reshape.141
  33.8 0.7 copy-done.8
  34.5 0.6 convolution_convert_fusion
  36.2 1.0 copy.11
  37.2 1.0 copy.12
  38.2 0.9 pad.9
  39.2 1.5 reshape.140
  41.0 0.7 copy-done.6
  41.7 0.6 convolution_convert_fusion.2
  42.7 0.6 convolution_convert_fusion.3
  43.7 0.7 copy-done.2
  45.5 0.7 copy-done.1
  46.2 1.3 fusion.2
  47.5 138.6 %all-reduce.5.cloned.1.call-done = (f32[128,2048]{1,0:T(8,128)}, f32[128,2048]{1,0:T(8,128)}) async-done(((f32[128,2048]{1,0:T(8,128)}, f32[128,2048]{1,0:T(8,128)}), (f32[128,2048]{1,0:T(8,128)}, f32[128,2048]{1,0:T(8,128)})) %all-reduce.5.cloned.1.call-update) | async-done | bytes 2097168 | tf_op jit(solution)/shard_map/psum | solution.py:78
  186.2 1.7 maximum_divide_fusion
  (44 shorter events, 4.4 us)
Async XLA Ops:
  7.2 12.8 %copy-start = (f32[16,21]{1,0:T(8,128)S(1)}, f32[16,21]{1,0:T(8,128)}, u32[]{:S(2)}) copy-start(f32[16,21]{1,0:T(8,128)} %param.10) | copy-start | bytes 4036
  7.2 13.0 %copy-start.10 = (f32[2]{0:T(128)S(1)}, f32[2]{0:T(128)}, u32[]{:S(2)}) copy-start(f32[2]{0:T(128)} %constant.35.clone) | copy-start | bytes 28
  7.2 12.8 %copy-start.9 = (s32[2,2,2]{2,1,0:T(2,128)S(1)}, s32[2,2,2]{2,1,0:T(2,128)}, u32[]{:S(2)}) copy-start(s32[2,2,2]{2,1,0:T(2,128)} %param.9) | copy-start | bytes 100
  7.2 179.0 %all-reduce.5.cloned.1.call-start = ((), (), s32[]{:S(2)}) async-start(), calls=%async_computation | async-start | bytes 4194304 | tf_op jit(solution)/shard_map/psum | solution.py:78
  8.3 12.2 %copy-start.4 = (bf16[2,128,2048]{2,1,0:T(8,128)(2,1)S(1)}, bf16[2,128,2048]{2,1,0:T(8,128)(2,1)}, u32[]{:S(2)}) copy-start(bf16[2,128,2048]{2,1,0:T(8,128)(2,1)} %param.7) | copy-start | bytes 3145732
  9.8 20.0 %collective-permute-start = (bf16[2,10,2048]{2,1,0:T(8,128)(2,1)S(1)}, bf16[2,10,2048]{2,1,0:T(8,128)(2,1)S(1)}, u32[]{:S(2)}, u32[]{:S(2)}) collective-permute-start(bf16[2,10,2048]{2,1,0:T(8,128)(2,1)S(1)} %get-tuple-element.26), channel_id=1, source_target_pairs={{0,32},{32,64},{64,96},{96,128},{128,160},{160,192},{192,224},{224... | collective-permute-start | bytes 245768 | tf_op jit(solution)/shard_map/ppermute | solution.py:19
  15.2 14.6 %collective-permute-start.1 = (bf16[2,10,2048]{2,1,0:T(8,128)(2,1)S(1)}, bf16[2,10,2048]{2,1,0:T(8,128)(2,1)S(1)}, u32[]{:S(2)}, u32[]{:S(2)}) collective-permute-start(bf16[2,10,2048]{2,1,0:T(8,128)(2,1)S(1)} %get-tuple-element.27), channel_id=1, source_target_pairs={{32,0},{64,32},{96,64},{128,96},{160,128},{192,160},{224,192},{256... | collective-permute-start | bytes 245768 | tf_op jit(solution)/shard_map/ppermute | solution.py:20
  33.5 1.0 copy-start.8
  34.5 1.0 copy-start.7
  36.2 2.0 %copy-start.3 = (bf16[148,2048]{1,0:T(8,128)(2,1)S(1)}, bf16[148,2048]{1,0:T(8,128)(2,1)}, u32[]{:S(2)}) copy-start(bf16[148,2048]{1,0:T(8,128)(2,1)} %get-tuple-element.17) | copy-start | bytes 1818628
  40.7 1.0 copy-start.6
  41.7 1.0 copy-start.5
  43.4 1.1 copy-start.2
  45.1 1.1 copy-start.1
Sparse Core Ops, SparseCore 0:
  47.7 138.4 all-reduce.4
where the time goes:
time: 198 us; the launch traced here: 195 us
  waiting for transfers between devices  139 us (70%)
  between operations  14.4 us (7%)
  other arithmetic  14.1 us (7%)
  local copies, waits for them, and re-layouts  12.4 us (6%)
  starting transfers between devices  10.1 us (5%)
  matrix products  5.07 us (3%)
    psum x1, waiting for transfers between devices, shards(): numer_full, denom_full = lax.psum((numer, denom), 'epoch')  139 us
    reduce_sum x2, other arithmetic, band_matrix(): jnp.sum(jnp.where(picks, taps_row.astype(jnp.float32), 0.0), axis=-1)  8.03 us
    unnamed x30, local copies, waits for them, and re-layouts  5.93 us
    ppermute x1, starting transfers between devices, with_halo(): before = lax.ppermute(last, axis, up)  5.39 us
    ppermute x1, starting transfers between devices, with_halo(): after = lax.ppermute(initial, axis, down)  4.69 us
  transfers between devices with their start and end apart: 3, of which 1 were waited for; matrix products, arithmetic and copies ran while one was open for 5% of the time, Pallas kernels for 0%

commit v1 on v0

v1 whole, which is shorter than its diff:
```python
import functools

import jax
import jax.numpy as jnp
from jax import lax
from jax.experimental import pallas as pl
from jax.experimental.pallas import tpu as pltpu
from jax.sharding import PartitionSpec as P

UNIT = 128
HALF = 10
TAPS = 21
NCOMP = 2
LANES = 128
EDGE = 16
TRANSPOSED = (((1,), (1,)), ((), ()))


def toeplitz(base, rows, shift):
    width = base.shape[1]
    wide = jnp.broadcast_to(base, (rows, width))
    if shift:
        wide = pltpu.roll(wide, shift % width, 1)
    return pltpu.roll(wide, 0, 1, stride=1, stride_axis=0)


def matrices(index_ref, bank_ref, row_ref, own_ref, edge_ref):
    exp_count = row_ref.shape[0]
    lane = lax.broadcasted_iota(jnp.int32, (EDGE, LANES), 1)
    for exp in range(exp_count):
        edge_top = jnp.zeros((EDGE, LANES), jnp.float32)
        edge_bottom = jnp.zeros((EDGE, LANES), jnp.float32)
        for comp in range(NCOMP):
            bases = []
            for side in range(2):
                taps = bank_ref[pl.ds(index_ref[exp, 2 * comp + side], 1), :]
                taps = taps / jnp.sum(taps, axis=1, keepdims=True)
                if side == 1:
                    taps = taps * (1.0 / NCOMP)
                taps = taps.astype(jnp.bfloat16).astype(jnp.float32)
                bases.append(
                    jnp.concatenate([taps, jnp.zeros((1, 2 * LANES - TAPS), jnp.float32)], axis=1)
                )
            row_ref[exp, comp * LANES : (comp + 1) * LANES, :] = toeplitz(bases[0], LANES, 0).astype(jnp.bfloat16)
            wide = toeplitz(bases[1], UNIT, -HALF)
            own_ref[exp, :, comp * UNIT : (comp + 1) * UNIT] = wide[:, :UNIT].astype(jnp.bfloat16)
            short = bases[1][:, :LANES]
            first = comp * EDGE
            top = toeplitz(short, EDGE, first + EDGE - HALF)
            edge_top = jnp.where((lane >= first) & (lane < first + EDGE), top, edge_top)
            first = (NCOMP + comp) * EDGE
            bottom = toeplitz(short, EDGE, first - EDGE - HALF)
            edge_bottom = jnp.where((lane >= first) & (lane < first + EDGE), bottom, edge_bottom)
        edge_ref[exp, :EDGE, :] = edge_top.astype(jnp.bfloat16)
        edge_ref[exp, EDGE:, :] = edge_bottom.astype(jnp.bfloat16)


def partial_sums(
    bounds_ref, place_ref, pixels_ref, above_ref, below_ref, variance_ref, row_ref, own_ref, edge_ref,
    out_ref, window_ref, across_ref, halo_ref, numer_ref, denom_ref,
):
    exp = pl.program_id(0)
    last = pl.num_programs(0) - 1
    unit = place_ref[0]
    lower, upper = bounds_ref[exp, 0], bounds_ref[exp, 1]

    def covers(at):
        return jnp.where((at >= lower) & (at < upper), 1.0, 0.0)

    width = pixels_ref.shape[2]
    blocks = width // LANES
    rows = UNIT + 2 * EDGE
    pixels = jnp.concatenate(
        [
            pixels_ref[0].astype(jnp.float32),
            above_ref[0].astype(jnp.float32) * covers(unit - 1),
            below_ref[0].astype(jnp.float32) * covers(unit + 1),
        ],
        axis=0,
    )
    moved = pltpu.roll(pixels, HALF, 1)
    lane = lax.broadcasted_iota(jnp.int32, (rows, LANES), 1)
    head = moved[:, :LANES]
    window_ref[:, :LANES] = jnp.where(lane < HALF, 0.0, head).astype(jnp.bfloat16)
    window_ref[:, LANES:width] = moved[:, LANES:].astype(jnp.bfloat16)
    window_ref[:, width:] = jnp.where(lane < HALF, head, 0.0).astype(jnp.bfloat16)
    for block in range(blocks):
        at = slice(block * LANES, (block + 1) * LANES)
        filtered = lax.dot_general(
            window_ref[:, block * LANES : (block + 2) * LANES],
            row_ref[0],
            TRANSPOSED,
            preferred_element_type=jnp.float32,
        ).astype(jnp.bfloat16)
        for comp in range(NCOMP):
            mine = filtered[:, comp * LANES : (comp + 1) * LANES]
            across_ref[comp * UNIT : (comp + 1) * UNIT, at] = mine[:UNIT]
            halo_ref[comp * EDGE : (comp + 1) * EDGE, at] = mine[UNIT : UNIT + EDGE]
            first = (NCOMP + comp) * EDGE
            halo_ref[first : first + EDGE, at] = mine[UNIT + EDGE :]
    weights = variance_ref[0].astype(jnp.float32) * covers(unit)
    smoothed = jnp.dot(own_ref[0], across_ref[...], preferred_element_type=jnp.float32)
    edges = jnp.dot(
        edge_ref[0, :, : 2 * NCOMP * EDGE], halo_ref[...], preferred_element_type=jnp.float32
    )
    smoothed = jnp.concatenate(
        [smoothed[:EDGE] + edges[:EDGE], smoothed[EDGE : UNIT - EDGE], smoothed[UNIT - EDGE :] + edges[EDGE:]],
        axis=0,
    )
    term = weights * smoothed

    @pl.when(exp == 0)
    def _():
        numer_ref[...] = term
        denom_ref[...] = weights

    @pl.when(exp > 0)
    def _():
        numer_ref[...] += term
        denom_ref[...] += weights

    @pl.when(exp == last)
    def _():
        parts, _, share = out_ref.shape
        for part in range(parts):
            at = slice(part * share, (part + 1) * share)
            out_ref[part, :UNIT, :] = numer_ref[:, at].astype(jnp.bfloat16)
            out_ref[part, UNIT:, :] = denom_ref[:, at].astype(jnp.bfloat16)


def finish(parts_ref, coadd_ref, depth_ref):
    numer = jnp.sum(parts_ref[:, :UNIT, :].astype(jnp.float32), axis=0)
    denom = jnp.sum(parts_ref[:, UNIT:, :].astype(jnp.float32), axis=0)
    coadd_ref[...] = numer / jnp.maximum(denom, 1.0)
    depth_ref[...] = denom


def whole(shape):
    return pl.BlockSpec(shape, lambda *_: (0,) * len(shape))


def each(shape):
    return pl.BlockSpec((1,) + shape[1:], lambda exp: (exp,) + (0,) * (len(shape) - 1))


def shards(exposures, inv_variance, strip_bounds, kernel_index, basis_bank):
    exp_count, row_count, width = exposures.shape
    patches, parts = lax.axis_size("patch"), lax.axis_size("epoch")
    share = width // parts
    down = [(i, i + 1) for i in range(patches - 1)]
    up = [(i + 1, i) for i in range(patches - 1)]
    above = lax.ppermute(exposures[:, row_count - EDGE :], "patch", down)
    below = lax.ppermute(exposures[:, :EDGE], "patch", up)
    smem = pl.BlockSpec(memory_space=pltpu.SMEM)
    row_mats, own_mats, edge_mats = pl.pallas_call(
        matrices,
        out_shape=(
            jax.ShapeDtypeStruct((exp_count, NCOMP * LANES, 2 * LANES), jnp.bfloat16),
            jax.ShapeDtypeStruct((exp_count, UNIT, NCOMP * UNIT), jnp.bfloat16),
            jax.ShapeDtypeStruct((exp_count, 2 * EDGE, LANES), jnp.bfloat16),
        ),
        in_specs=[smem, whole(basis_bank.shape)],
        name="band_matrices",
    )(kernel_index.reshape(exp_count, 2 * NCOMP), basis_bank)
    place = lax.axis_index("patch").reshape(1).astype(jnp.int32)
    sums = pl.pallas_call(
        partial_sums,
        out_shape=jax.ShapeDtypeStruct((parts, 2 * row_count, share), jnp.bfloat16),
        grid=(exp_count,),
        in_specs=[
            smem,
            smem,
            each(exposures.shape),
            each(above.shape),
            each(below.shape),
            each(inv_variance.shape),
            each(row_mats.shape),
            each(own_mats.shape),
            each(edge_mats.shape),
        ],
        out_specs=whole((parts, 2 * row_count, share)),
        scratch_shapes=[
            pltpu.VMEM((UNIT + 2 * EDGE, width + LANES), jnp.bfloat16),
            pltpu.VMEM((NCOMP * UNIT, width), jnp.bfloat16),
            pltpu.VMEM((2 * NCOMP * EDGE, width), jnp.bfloat16),
            pltpu.VMEM((row_count, width), jnp.float32),
            pltpu.VMEM((row_count, width), jnp.float32),
        ],
        compiler_params=pltpu.CompilerParams(vmem_limit_bytes=32 * 1024 * 1024),
        name="partial_sums",
    )(strip_bounds, place, exposures, above, below, inv_variance, row_mats, own_mats, edge_mats)
    received = lax.all_to_all(sums, "epoch", 0, 0, tiled=True)
    out = jax.ShapeDtypeStruct((row_count, share), jnp.float32)
    return pl.pallas_call(finish, out_shape=(out, out), name="finish")(received)


def solution(mesh):
    return jax.shard_map(
        shards,
        mesh=mesh,
        in_specs=(
            P(("band", "epoch"), "patch", None),
            P(("band", "epoch"), "patch", None),
            P(("band", "epoch"), None),
            P(("band", "epoch"), None, None),
            P(),
        ),
        out_specs=(P(("band", "patch"), "epoch"), P(("band", "patch"), "epoch")),
        check_vma=False,
    )
```

time: 198 us -> 61.8 us (0.31)
  the two profiles are of different devices: /device:TPU:1 before, /device:TPU:201 now
where the time goes in v1:
time: 61.8 us; the launch traced here: 61.3 us
  blocking collectives  37.6 us (61%)
  local copies, waits for them, and re-layouts  8.02 us (13%)
  starting transfers between devices  7.69 us (12%)
  Pallas kernels  7.27 us (12%)
  between operations  0.69 us (1%)
    all_to_all x1, blocking collectives, shards(): received = lax.all_to_all(sums, 'epoch', 0, 0, tiled=True)  37.6 us
    unnamed x14, local copies, waits for them, and re-layouts  6.37 us
    ppermute x1, starting transfers between devices, shards(): above = lax.ppermute(exposures[:, row_count - EDGE:], 'patch', down)  5.11 us
    pallas_call x1, Pallas kernels, shards(): pl.pallas_call(partial_sums, out_shape=jax.ShapeDtypeStruct((parts, 2 * r...  3.23 us
    ppermute x1, starting transfers between devices, shards(): below = lax.ppermute(exposures[:, :EDGE], 'patch', up)  2.58 us
    pallas_call x1, Pallas kernels, shards(): return pl.pallas_call(finish, out_shape=(out, out), name='finish')(received)  2.07 us
    pallas_call x1, Pallas kernels, shards(): pl.pallas_call(matrices, out_shape=(jax.ShapeDtypeStruct((exp_count, NCOM...  1.97 us
  transfers between devices with their start and end apart: 2, of which 0 were waited for; matrix products, arithmetic and copies ran while one was open for 1% of the time, Pallas kernels for 3%

profile of v1, /device:TPU:201, one launch (start us, length us, event | category | flops | bytes accessed | tf_op | source)
XLA Modules:
  0.0 61.3 jit_solution(13855211269490368071)
XLA Ops:
  0.6 1.0 %fusion = (bf16[2,16,2048]{2,1,0:T(8,128)(2,1)S(1)}, bf16[2,16,2048]{2,1,0:T(8,128)(2,1)S(1)}) fusion(bf16[2,128,2048]{2,1,0:T(8,128)(2,1)} %pixels_ref.1), kind=kLoop, calls=%fused_computation | loop fusion | bytes 524288 | tf_op jit(solution)/shard_map/slice | solution.py:153
  1.6 2.6 %collective-permute-start.1 = (bf16[2,16,2048]{2,1,0:T(8,128)(2,1)S(1)}, bf16[2,16,2048]{2,1,0:T(8,128)(2,1)S(1)}, u32[]{:S(2)}, u32[]{:S(2)}) collective-permute-start(bf16[2,16,2048]{2,1,0:T(8,128)(2,1)S(1)} %get-tuple-element.8), channel_id=1, source_target_pairs={{32,0},{64,32},{96,64},{128,96},{160,128},{192,160},{224,192},{256... | collective-permute-start | bytes 393224 | tf_op jit(solution)/shard_map/ppermute | solution.py:153
  4.2 5.1 %collective-permute-start = (bf16[2,16,2048]{2,1,0:T(8,128)(2,1)S(1)}, bf16[2,16,2048]{2,1,0:T(8,128)(2,1)S(1)}, u32[]{:S(2)}, u32[]{:S(2)}) collective-permute-start(bf16[2,16,2048]{2,1,0:T(8,128)(2,1)S(1)} %get-tuple-element.9), channel_id=1, source_target_pairs={{0,32},{32,64},{64,96},{96,128},{128,160},{160,192},{192,224},{224... | collective-permute-start | bytes 393224 | tf_op jit(solution)/shard_map/ppermute | solution.py:152
  9.3 0.0 copy-start.6
  9.3 0.7 %copy-done.6 = s32[2,2,2]{2,1,0:T(2,128)S(1)} copy-done((s32[2,2,2]{2,1,0:T(2,128)S(1)}, s32[2,2,2]{2,1,0:T(2,128)}, u32[]{:S(2)}) %copy-start.6) | copy-done | bytes 56
  10.0 0.7 %reshape.11.index_ref = s32[2,4]{1,0:T(2,128)} reshape(s32[2,2,2]{2,1,0:T(2,128)S(1)} %copy-done.6) | data formatting | bytes 64 | tf_op jit(solution)/shard_map/reshape | solution.py:164
  10.7 2.0 %band_matrices.1 = (bf16[2,256,256]{2,1,0:T(8,128)(2,1)}, bf16[2,128,256]{2,1,0:T(8,128)(2,1)}, bf16[2,32,128]{2,1,0:T(8,128)(2,1)}) custom-call(s32[2,4]{1,0:T(2,128)} %reshape.11.index_ref, f32[16,21]{1,0:T(8,128)} %bank_ref.1), custom_call_target="tpu_custom_call" | custom-call | tf_op jit(solution)/shard_map/band_matrices/pallas_call | solution.py:155
  12.6 0.0 collective-permute-done.1.below_ref
  12.7 0.0 collective-permute-done.above_ref
  12.7 0.0 copy-start.5
  12.7 0.7 %copy-done.5 = s32[2,2]{1,0:T(2,128)S(1)} copy-done((s32[2,2]{1,0:T(2,128)S(1)}, s32[2,2]{1,0:T(2,128)}, u32[]{:S(2)}) %copy-start.5) | copy-done | bytes 40
  13.3 0.0 copy-start
  13.3 1.2 %copy-done = bf16[2,128,2048]{2,1,0:T(8,128)(2,1)S(1)} copy-done((bf16[2,128,2048]{2,1,0:T(8,128)(2,1)S(1)}, bf16[2,128,2048]{2,1,0:T(8,128)(2,1)}, u32[]{:S(2)}) %copy-start) | copy-done | bytes 1048600
  14.6 0.0 copy-start.1
  14.6 1.2 %copy-done.1 = bf16[2,128,2048]{2,1,0:T(8,128)(2,1)S(1)} copy-done((bf16[2,128,2048]{2,1,0:T(8,128)(2,1)S(1)}, bf16[2,128,2048]{2,1,0:T(8,128)(2,1)}, u32[]{:S(2)}) %copy-start.1) | copy-done | bytes 1048600
  15.8 0.0 copy-start.2
  15.8 0.9 %copy-done.2 = bf16[2,256,256]{2,1,0:T(8,128)(2,1)S(1)} copy-done((bf16[2,256,256]{2,1,0:T(8,128)(2,1)S(1)}, bf16[2,256,256]{2,1,0:T(8,128)(2,1)}, u32[]{:S(2)}) %copy-start.2) | copy-done | bytes 262168
  16.7 0.0 copy-start.3
  16.7 0.9 %copy-done.3 = bf16[2,128,256]{2,1,0:T(8,128)(2,1)S(1)} copy-done((bf16[2,128,256]{2,1,0:T(8,128)(2,1)S(1)}, bf16[2,128,256]{2,1,0:T(8,128)(2,1)}, u32[]{:S(2)}) %copy-start.3) | copy-done | bytes 131096
  17.6 0.0 copy-start.4
  17.6 0.7 %copy-done.4 = bf16[2,32,128]{2,1,0:T(8,128)(2,1)S(1)} copy-done((bf16[2,32,128]{2,1,0:T(8,128)(2,1)S(1)}, bf16[2,32,128]{2,1,0:T(8,128)(2,1)}, u32[]{:S(2)}) %copy-start.4) | copy-done | bytes 16408
  18.4 3.2 %partial_sums.1 = bf16[8,256,256]{2,1,0:T(8,128)(2,1)S(1)} custom-call(s32[2,2]{1,0:T(2,128)S(1)} %copy-done.5, s32[1]{0:T(128)} %bitcast.place_ref, bf16[2,128,2048]{2,1,0:T(8,128)(2,1)S(1)} %copy-done, bf16[2,16,2048]{2,1,0:T(8,128)(2,1)S(1)} %collective-permute-done.above_ref, bf16[2,16,2048]{2,1,0:T(8,128)(2,1)S(1)} %collective-permute-done.1.below_ref, ...), custom_call_target="tpu_custom_call" | custom-call | tf_op jit(solution)/shard_map/partial_sums/pallas_call | solution.py:166
  21.6 37.6 %all_to_all.5.parts_ref = bf16[8,256,256]{2,1,0:T(8,128)(2,1)} all-to-all(bf16[8,256,256]{2,1,0:T(8,128)(2,1)S(1)} %partial_sums.1), channel_id=1, replica_groups=mesh['patch'=16,'epoch'=8,'band'=4] {'epoch'}, dimensions={0} | all-to-all | bytes 2097152 | tf_op jit(solution)/shard_map/all_to_all | solution.py:192
  59.2 2.1 %finish.1 = (f32[128,256]{1,0:T(8,128)}, f32[128,256]{1,0:T(8,128)}) custom-call(bf16[8,256,256]{2,1,0:T(8,128)(2,1)} %all_to_all.5.parts_ref), custom_call_target="tpu_custom_call" | custom-call | tf_op jit(solution)/shard_map/finish/pallas_call | solution.py:194
Async XLA Ops:
  1.6 11.0 %collective-permute-start.1 = (bf16[2,16,2048]{2,1,0:T(8,128)(2,1)S(1)}, bf16[2,16,2048]{2,1,0:T(8,128)(2,1)S(1)}, u32[]{:S(2)}, u32[]{:S(2)}) collective-permute-start(bf16[2,16,2048]{2,1,0:T(8,128)(2,1)S(1)} %get-tuple-element.8), channel_id=1, source_target_pairs={{32,0},{64,32},{96,64},{128,96},{160,128},{192,160},{224,192},{256... | collective-permute-start | bytes 393224 | tf_op jit(solution)/shard_map/ppermute | solution.py:153
  4.2 8.4 %collective-permute-start = (bf16[2,16,2048]{2,1,0:T(8,128)(2,1)S(1)}, bf16[2,16,2048]{2,1,0:T(8,128)(2,1)S(1)}, u32[]{:S(2)}, u32[]{:S(2)}) collective-permute-start(bf16[2,16,2048]{2,1,0:T(8,128)(2,1)S(1)} %get-tuple-element.9), channel_id=1, source_target_pairs={{0,32},{32,64},{64,96},{96,128},{128,160},{160,192},{192,224},{224... | collective-permute-start | bytes 393224 | tf_op jit(solution)/shard_map/ppermute | solution.py:152
  9.3 0.7 %copy-start.6 = (s32[2,2,2]{2,1,0:T(2,128)S(1)}, s32[2,2,2]{2,1,0:T(2,128)}, u32[]{:S(2)}) copy-start(s32[2,2,2]{2,1,0:T(2,128)} %param.8) | copy-start | bytes 100
  12.7 0.7 %copy-start.5 = (s32[2,2]{1,0:T(2,128)S(1)}, s32[2,2]{1,0:T(2,128)}, u32[]{:S(2)}) copy-start(s32[2,2]{1,0:T(2,128)} %bounds_ref.1) | copy-start | bytes 52
  13.3 1.2 %copy-start = (bf16[2,128,2048]{2,1,0:T(8,128)(2,1)S(1)}, bf16[2,128,2048]{2,1,0:T(8,128)(2,1)}, u32[]{:S(2)}) copy-start(bf16[2,128,2048]{2,1,0:T(8,128)(2,1)} %pixels_ref.1) | copy-start | bytes 3145732
  14.6 1.2 %copy-start.1 = (bf16[2,128,2048]{2,1,0:T(8,128)(2,1)S(1)}, bf16[2,128,2048]{2,1,0:T(8,128)(2,1)}, u32[]{:S(2)}) copy-start(bf16[2,128,2048]{2,1,0:T(8,128)(2,1)} %variance_ref.1) | copy-start | bytes 3145732
  15.8 0.9 %copy-start.2 = (bf16[2,256,256]{2,1,0:T(8,128)(2,1)S(1)}, bf16[2,256,256]{2,1,0:T(8,128)(2,1)}, u32[]{:S(2)}) copy-start(bf16[2,256,256]{2,1,0:T(8,128)(2,1)} %get-tuple-element.5.row_ref) | copy-start | bytes 786436
  16.7 0.9 %copy-start.3 = (bf16[2,128,256]{2,1,0:T(8,128)(2,1)S(1)}, bf16[2,128,256]{2,1,0:T(8,128)(2,1)}, u32[]{:S(2)}) copy-start(bf16[2,128,256]{2,1,0:T(8,128)(2,1)} %get-tuple-element.6.own_ref) | copy-start | bytes 393220
  17.6 0.7 %copy-start.4 = (bf16[2,32,128]{2,1,0:T(8,128)(2,1)S(1)}, bf16[2,32,128]{2,1,0:T(8,128)(2,1)}, u32[]{:S(2)}) copy-start(bf16[2,32,128]{2,1,0:T(8,128)(2,1)} %get-tuple-element.7.edge_ref) | copy-start | bytes 49156

commit v2 on v0

v2 whole, which is shorter than its diff:
```python
import jax
import jax.numpy as jnp
from jax import lax
from jax.experimental import pallas as pl
from jax.experimental.pallas import tpu as pltpu
from jax.sharding import PartitionSpec as P

UNIT = 128
HALF = 10
TAPS = 21
NCOMP = 2
LANES = 128
EDGE = 16
FAR = 2
GROUP = 4
CHUNK = 32
TRANSPOSED = (((1,), (1,)), ((), ()))


def toeplitz(base, rows, shift):
    width = base.shape[1]
    if shift:
        base = pltpu.roll(base, shift % width, 1)
    return pltpu.roll(jnp.broadcast_to(base, (rows, width)), 0, 1, stride=1, stride_axis=0)


def matrices(index_ref, exp, taps_ref, row_ref, own_ref, edge_ref):
    lane = lax.broadcasted_iota(jnp.int32, (EDGE, LANES), 1)
    edge_top = jnp.zeros((EDGE, LANES), jnp.float32)
    edge_bottom = jnp.zeros((EDGE, LANES), jnp.float32)
    for comp in range(NCOMP):
        base = taps_ref[pl.ds(index_ref[exp, comp, 0], 1), :]
        row_ref[exp, comp * LANES : (comp + 1) * LANES, :] = toeplitz(base, LANES, 0).astype(jnp.bfloat16)
        base = taps_ref[pl.ds(index_ref[exp, comp, 1], 1), :] * (1.0 / NCOMP)
        wide = toeplitz(base, UNIT, -HALF)
        own_ref[exp, :, comp * UNIT : (comp + 1) * UNIT] = wide[:, :UNIT].astype(jnp.bfloat16)
        short = base[:, :LANES]
        first = comp * EDGE
        top = toeplitz(short, EDGE, first + EDGE - HALF)
        edge_top = jnp.where((lane >= first) & (lane < first + EDGE), top, edge_top)
        first = (NCOMP + comp) * EDGE
        bottom = toeplitz(short, EDGE, first - EDGE - HALF)
        edge_bottom = jnp.where((lane >= first) & (lane < first + EDGE), bottom, edge_bottom)
    edge_ref[exp, :EDGE, :] = edge_top.astype(jnp.bfloat16)
    edge_ref[exp, EDGE:, :] = edge_bottom.astype(jnp.bfloat16)


def mask(bounds_ref, exp, unit):
    return jnp.where((unit >= bounds_ref[exp, 0]) & (unit < bounds_ref[exp, 1]), 1.0, 0.0)


def fill_window(window_ref, exp, pixels):
    rows, width = pixels.shape
    moved = pltpu.roll(pixels, HALF, 1)
    lane = lax.broadcasted_iota(jnp.int32, (rows, LANES), 1)
    head = moved[:, :LANES]
    window_ref[exp, :, :LANES] = jnp.where(lane < HALF, 0.0, head).astype(jnp.bfloat16)
    window_ref[exp, :, LANES:width] = moved[:, LANES:].astype(jnp.bfloat16)
    window_ref[exp, :, width:] = jnp.where(lane < HALF, head, 0.0).astype(jnp.bfloat16)


def row_filter(window_ref, exp, matrix, start, count):
    stacked = jnp.concatenate(
        [window_ref[exp, :, block * LANES : (block + 2) * LANES] for block in range(start, start + count)], axis=0
    )
    return lax.dot_general(stacked, matrix, TRANSPOSED, preferred_element_type=jnp.float32).astype(jnp.bfloat16)


def spread(out_ref, value, rows=slice(None)):
    near, _, _, share = out_ref.shape
    for part in range(value.shape[1] // share):
        y, x = divmod(part, near)
        out_ref[x, y, rows, :] = value[:, part * share : (part + 1) * share].astype(out_ref.dtype)


def weight_sums(
    bounds_hbm, pixels_hbm, variance_hbm, denom_hbm, first_hbm, last_hbm,
    bounds_ref, first_ref, last_ref, variance_ref, denom_ref, in_sems, out_sems, side_sems,
):
    unit = lax.axis_index("patch")
    exp_count, rows, _ = variance_ref.shape
    chunks = [pl.ds(at, CHUNK) for at in range(0, rows, CHUNK)]
    sides = [
        pltpu.make_async_copy(bounds_hbm, bounds_ref, side_sems.at[0]),
        pltpu.make_async_copy(pixels_hbm.at[:, pl.ds(0, EDGE)], first_ref, side_sems.at[1]),
        pltpu.make_async_copy(pixels_hbm.at[:, pl.ds(rows - EDGE, EDGE)], last_ref, side_sems.at[2]),
    ]
    strips = [
        pltpu.make_async_copy(first_ref, first_hbm, side_sems.at[3]),
        pltpu.make_async_copy(last_ref, last_hbm, side_sems.at[4]),
    ]
    arrivals = [
        pltpu.make_async_copy(variance_hbm.at[:, at], variance_ref.at[:, at], in_sems.at[i])
        for i, at in enumerate(chunks)
    ]
    leaves = [
        pltpu.make_async_copy(denom_ref.at[:, :, at], denom_hbm.at[:, :, at], out_sems.at[i])
        for i, at in enumerate(chunks)
    ]
    for copy in sides + arrivals:
        copy.start()
    for copy in sides:
        copy.wait()
    for copy in strips:
        copy.start()
    masks = [mask(bounds_ref, exp, unit) for exp in range(exp_count)]
    for i, at in enumerate(chunks):
        arrivals[i].wait()
        denom = variance_ref[0, at, :].astype(jnp.float32) * masks[0]
        for exp in range(1, exp_count):
            denom += variance_ref[exp, at, :].astype(jnp.float32) * masks[exp]
        spread(denom_ref, denom, at)
        leaves[i].start()
    for copy in leaves + strips:
        copy.wait()


def weighted_sums(
    index_hbm, bounds_hbm, bank_hbm, above_hbm, below_hbm, pixels_hbm, variance_hbm, out_hbm,
    index_ref, bounds_ref, bank_ref, above_ref, below_ref,
    out_ref, taps_ref, row_ref, own_ref, edge_ref, pixels_ref, variance_ref, window_ref, across_ref, halo_ref,
    sems, side_sems, out_sems,
):
    unit = lax.axis_index("patch")
    exp_count, rows, width = pixels_ref.shape
    sides = [
        pltpu.make_async_copy(source, target, side_sems.at[i])
        for i, (source, target) in enumerate(
            (
                (index_hbm, index_ref),
                (bank_hbm, bank_ref),
                (bounds_hbm, bounds_ref),
                (above_hbm, above_ref),
                (below_hbm, below_ref),
            )
        )
    ]
    pixel_copies = [pltpu.make_async_copy(pixels_hbm.at[e], pixels_ref.at[e], sems.at[e]) for e in range(exp_count)]
    weight_copies = [
        pltpu.make_async_copy(variance_hbm.at[e], variance_ref.at[e], sems.at[exp_count + e]) for e in range(exp_count)
    ]
    for copy in sides:
        copy.start()
    for pair in zip(pixel_copies, weight_copies):
        for copy in pair:
            copy.start()
    for copy in sides:
        copy.wait()
    bank = bank_ref[...]
    bank = (bank / jnp.sum(bank, axis=1, keepdims=True)).astype(jnp.bfloat16).astype(jnp.float32)
    taps_ref[...] = jnp.concatenate([bank, jnp.zeros((bank.shape[0], 2 * LANES - TAPS), jnp.float32)], axis=1)
    for exp in range(exp_count):
        matrices(index_ref, exp, taps_ref, row_ref, own_ref, edge_ref)
    total = rows + 2 * EDGE
    for exp in range(exp_count):
        pixel_copies[exp].wait()
        above = above_ref[exp].astype(jnp.float32) * mask(bounds_ref, exp, unit - 1)
        below = below_ref[exp].astype(jnp.float32) * mask(bounds_ref, exp, unit + 1)
        fill_window(window_ref, exp, jnp.concatenate([pixels_ref[exp].astype(jnp.float32), above, below], axis=0))
        for start in range(0, width // LANES, GROUP):
            filtered = row_filter(window_ref, exp, row_ref[exp], start, GROUP)
            for block in range(GROUP):
                at = slice((start + block) * LANES, (start + block + 1) * LANES)
                for comp in range(NCOMP):
                    mine = filtered[block * total : (block + 1) * total, comp * LANES : (comp + 1) * LANES]
                    across_ref[exp, comp * UNIT : (comp + 1) * UNIT, at] = mine[:UNIT]
                    halo_ref[exp, comp * EDGE : (comp + 1) * EDGE, at] = mine[UNIT : UNIT + EDGE]
                    first = (NCOMP + comp) * EDGE
                    halo_ref[exp, first : first + EDGE, at] = mine[UNIT + EDGE :]
    for copy in weight_copies:
        copy.wait()
    masks = [mask(bounds_ref, exp, unit) for exp in range(exp_count)]
    near, _, _, share = out_ref.shape
    leaves = []
    for part in range(width // share):
        y, x = divmod(part, near)
        at = slice(part * share, (part + 1) * share)
        numer = jnp.zeros((rows, share), jnp.float32)
        for exp in range(exp_count):
            smoothed = jnp.dot(own_ref[exp], across_ref[exp, :, at], preferred_element_type=jnp.float32)
            edges = jnp.dot(
                edge_ref[exp, :, : 2 * NCOMP * EDGE], halo_ref[exp, :, at], preferred_element_type=jnp.float32
            )
            smoothed = jnp.concatenate(
                [smoothed[:EDGE] + edges[:EDGE], smoothed[EDGE : UNIT - EDGE], smoothed[UNIT - EDGE :] + edges[EDGE:]],
                axis=0,
            )
            numer += variance_ref[exp, :, at].astype(jnp.float32) * masks[exp] * smoothed
        out_ref[x, y] = numer.astype(out_ref.dtype)
        leaves.append(pltpu.make_async_copy(out_ref.at[x, y], out_hbm.at[x, y], out_sems.at[part]))
        leaves[-1].start()
    for copy in leaves:
        copy.wait()


def shards(exposures, inv_variance, strip_bounds, kernel_index, basis_bank):
    exp_count, row_count, width = exposures.shape
    patches, parts = lax.axis_size("patch"), lax.axis_size("epoch")
    near = parts // FAR
    share = width // parts
    f32, bf16 = jnp.float32, jnp.bfloat16
    hbm = pl.BlockSpec(memory_space=pl.ANY)
    far = lax.axis_index("epoch") // near
    groups = [[y * near + x for x in range(near)] for y in range(FAR)]
    swap = [(at, (at + near) % parts) for at in range(parts)]
    sends = jax.ShapeDtypeStruct((near, FAR, row_count, share), bf16)
    strip = jax.ShapeDtypeStruct((exp_count, EDGE, width), bf16)

    def reduce_near(sums):
        received = lax.all_to_all(sums, "epoch", 0, 0, tiled=True, axis_index_groups=groups)
        halves = jnp.sum(received.astype(f32), axis=0)
        return jnp.where(far == 0, halves[0], halves[1]), jnp.where(far == 0, halves[1], halves[0]).astype(bf16)

    denom_sums, first, last = pl.pallas_call(
        weight_sums,
        out_shape=(sends, strip, strip),
        in_specs=[hbm] * 3,
        out_specs=(hbm,) * 3,
        scratch_shapes=[
            pltpu.SMEM(strip_bounds.shape, jnp.int32),
            pltpu.VMEM(strip.shape, bf16),
            pltpu.VMEM(strip.shape, bf16),
            pltpu.VMEM(inv_variance.shape, bf16),
            pltpu.VMEM(sends.shape, bf16),
            pltpu.SemaphoreType.DMA((row_count // CHUNK,)),
            pltpu.SemaphoreType.DMA((row_count // CHUNK,)),
            pltpu.SemaphoreType.DMA((5,)),
        ],
        name="weight_sums",
    )(strip_bounds, exposures, inv_variance)
    above = lax.ppermute(last, "patch", [(i, i + 1) for i in range(patches - 1)])
    below = lax.ppermute(first, "patch", [(i + 1, i) for i in range(patches - 1)])
    denom, denom_give = reduce_near(denom_sums)
    far_denom = lax.ppermute(denom_give, "epoch", swap)
    numer_sums = pl.pallas_call(
        weighted_sums,
        out_shape=sends,
        in_specs=[hbm] * 7,
        out_specs=hbm,
        scratch_shapes=[
            pltpu.SMEM(kernel_index.shape, jnp.int32),
            pltpu.SMEM(strip_bounds.shape, jnp.int32),
            pltpu.VMEM(basis_bank.shape, f32),
            pltpu.VMEM(strip.shape, bf16),
            pltpu.VMEM(strip.shape, bf16),
            pltpu.VMEM(sends.shape, bf16),
            pltpu.VMEM((basis_bank.shape[0], 2 * LANES), f32),
            pltpu.VMEM((exp_count, NCOMP * LANES, 2 * LANES), bf16),
            pltpu.VMEM((exp_count, UNIT, NCOMP * UNIT), bf16),
            pltpu.VMEM((exp_count, 2 * EDGE, LANES), bf16),
            pltpu.VMEM(exposures.shape, bf16),
            pltpu.VMEM(inv_variance.shape, bf16),
            pltpu.VMEM((exp_count, UNIT + 2 * EDGE, width + LANES), bf16),
            pltpu.VMEM((exp_count, NCOMP * UNIT, width), bf16),
            pltpu.VMEM((exp_count, 2 * NCOMP * EDGE, width), bf16),
            pltpu.SemaphoreType.DMA((2 * exp_count,)),
            pltpu.SemaphoreType.DMA((5,)),
            pltpu.SemaphoreType.DMA((parts,)),
        ],
        name="weighted_sums",
    )(kernel_index, strip_bounds, basis_bank, above, below, exposures, inv_variance)
    numer, numer_give = reduce_near(numer_sums)
    numer = numer + lax.ppermute(numer_give, "epoch", swap).astype(f32)
    denom = denom + far_denom.astype(f32)
    return numer / jnp.maximum(denom, 1.0), denom


def solution(mesh):
    return jax.shard_map(
        shards,
        mesh=mesh,
        in_specs=(
            P(("band", "epoch"), "patch", None),
            P(("band", "epoch"), "patch", None),
            P(("band", "epoch"), None),
            P(("band", "epoch"), None, None),
            P(),
        ),
        out_specs=(P(("band", "patch"), "epoch"), P(("band", "patch"), "epoch")),
        check_vma=False,
    )
```

time: 198 us -> 49.4 us (0.25); the launches traced: 195 us -> 49 us
  waiting for transfers between devices: 139 us -> 8.89 us
  starting transfers between devices: 10.1 us -> 31 us
  between operations: 14.4 us -> 0.75 us
  other arithmetic: 14.1 us -> 0.91 us
  local copies, waits for them, and re-layouts: 12.4 us -> 0.67 us
  Pallas kernels: 0 us -> 6.84 us
  matrix products: 5.07 us -> 0 us
    psum x1 -> x0, waiting for transfers between devices: 139 us -> none  [shards(): numer_full, denom_full = lax.psum((numer, denom), 'epoch')]
    ppermute x2 -> x4, starting transfers between devices: 10.1 us -> 21.7 us  [the longest x1 7.45 us: shards(): far_denom = lax.ppermute(denom_give, 'epoch', swap)]
    all_to_all x0 -> x2, starting transfers between devices: none -> 9.22 us  [reduce_near(): lax.all_to_all(sums, 'epoch', 0, 0, tiled=True, axis_index_groups=groups)]
    reduce_sum x2, other arithmetic: 8.03 us -> 0.15 us  [reduce_near(): halves = jnp.sum(received.astype(f32), axis=0)]
    ppermute x2 -> x4, waiting for transfers between devices: 0.01 us -> 7.07 us  [the longest x1 4.41 us: shards(): numer = numer + lax.ppermute(numer_give, 'epoch', swap).astype(f32)]
    pallas_call x0 -> x2, Pallas kernels: none -> 6.84 us  [the longest x1 4.65 us: shards(): pl.pallas_call(weighted_sums, out_shape=sends, in_specs=[hbm] * 7, out_sp...]
    unnamed x30 -> x8, local copies, waits for them, and re-layouts: 5.93 us -> 0.67 us
    dot_general x9 -> x0, matrix products: 5.07 us -> none  [the longest x4 2.55 us: horizontal(): jnp.einsum('rbi,ij->rbj', window, matrix, preferred_element_type=jnp.floa...]
  transfers between devices with their start and end apart: 3 -> 6, of which waited for: 1 -> 3; matrix products, arithmetic and copies ran while one was open for 5% -> 0% of each run, Pallas kernels for 0% -> 9%
where the time goes in v2:
time: 49.4 us; the launch traced here: 49 us
  starting transfers between devices  31 us (63%)
  waiting for transfers between devices  8.89 us (18%)
  Pallas kernels  6.84 us (14%)
  other arithmetic  0.91 us (2%)
  between operations  0.75 us (2%)
  local copies, waits for them, and re-layouts  0.67 us (1%)
    all_to_all x2, starting transfers between devices, reduce_near(): lax.all_to_all(sums, 'epoch', 0, 0, tiled=True, axis_index_groups=groups)  9.22 us
    ppermute x1, starting transfers between devices, shards(): far_denom = lax.ppermute(denom_give, 'epoch', swap)  7.45 us
    ppermute x1, starting transfers between devices, shards(): numer = numer + lax.ppermute(numer_give, 'epoch', swap).astype(f32)  5.57 us
    ppermute x1, starting transfers between devices, shards(): lax.ppermute(last, 'patch', [(i, i + 1) for i in range(patches - 1)])  4.83 us
    pallas_call x1, Pallas kernels, shards(): pl.pallas_call(weighted_sums, out_shape=sends, in_specs=[hbm] * 7, out_sp...  4.65 us
    ppermute x1, waiting for transfers between devices, shards(): numer = numer + lax.ppermute(numer_give, 'epoch', swap).astype(f32)  4.41 us
    ppermute x1, starting transfers between devices, shards(): lax.ppermute(first, 'patch', [(i + 1, i) for i in range(patches - 1)])  3.9 us
    ppermute x1, waiting for transfers between devices, shards(): lax.ppermute(first, 'patch', [(i + 1, i) for i in range(patches - 1)])  2.65 us
  transfers between devices with their start and end apart: 6, of which 3 were waited for; matrix products, arithmetic and copies ran while one was open for 0% of the time, Pallas kernels for 9%

profile of v2, /device:TPU:1, one launch (start us, length us, event | category | flops | bytes accessed | tf_op | source)
XLA Modules:
  0.0 49.0 jit_solution(9233303937548125676)
XLA Ops:
  0.6 2.2 %weight_sums.1 = (bf16[4,2,128,256]{3,2,1,0:T(8,128)(2,1)}, bf16[2,16,2048]{2,1,0:T(8,128)(2,1)}, bf16[2,16,2048]{2,1,0:T(8,128)(2,1)}) custom-call(s32[2,2]{1,0:T(2,128)} %bounds_hbm.3, bf16[2,128,2048]{2,1,0:T(8,128)(2,1)} %pixels_hbm.3, bf16[2,128,2048]{2,1,0:T(8,128)(2,1)} %variance_hbm.3), custom_call_target="tpu_custom_call" | custom-call | tf_op jit(solution)/shard_map/weight_sums/pallas_call | solution.py:214
  2.8 0.0 copy-start.3
  2.8 0.0 copy-start.2
  2.8 5.0 %all-to-all-start.1 = ((bf16[4,2,128,256]{3,2,1,0:T(8,128)(2,1)}), bf16[4,2,128,256]{3,2,1,0:T(8,128)(2,1)S(1)}, u32[]{:S(2)}, u32[]{:S(2)}) async-start(bf16[4,2,128,256]{3,2,1,0:T(8,128)(2,1)} %get-tuple-element.7), calls=%async_computation.1 | async-start | bytes 1048576 | tf_op jit(solution)/shard_map/all_to_all | solution.py:210
  7.8 0.0 copy-done.3
  7.8 4.8 %collective-permute-start = (bf16[2,16,2048]{2,1,0:T(8,128)(2,1)S(1)}, bf16[2,16,2048]{2,1,0:T(8,128)(2,1)S(1)}, u32[]{:S(2)}, u32[]{:S(2)}) collective-permute-start(bf16[2,16,2048]{2,1,0:T(8,128)(2,1)S(1)} %copy-done.3), channel_id=1, source_target_pairs={{0,32},{32,64},{64,96},{96,128},{128,160},{160,192},{192,224},{224... | collective-permute-start | bytes 393224 | tf_op jit(solution)/shard_map/ppermute | solution.py:231
  12.7 0.0 copy-done.2
  12.7 3.9 %collective-permute-start.1 = (bf16[2,16,2048]{2,1,0:T(8,128)(2,1)S(1)}, bf16[2,16,2048]{2,1,0:T(8,128)(2,1)S(1)}, u32[]{:S(2)}, u32[]{:S(2)}) collective-permute-start(bf16[2,16,2048]{2,1,0:T(8,128)(2,1)S(1)} %copy-done.2), channel_id=1, source_target_pairs={{32,0},{64,32},{96,64},{128,96},{160,128},{192,160},{224,192},{256... | collective-permute-start | bytes 393224 | tf_op jit(solution)/shard_map/ppermute | solution.py:232
  16.6 0.0 collective-permute-done.above_hbm
  16.6 0.0 copy-start
  16.6 2.7 %collective-permute-done.1.below_hbm = bf16[2,16,2048]{2,1,0:T(8,128)(2,1)S(1)} collective-permute-done((bf16[2,16,2048]{2,1,0:T(8,128)(2,1)S(1)}, bf16[2,16,2048]{2,1,0:T(8,128)(2,1)S(1)}, u32[]{:S(2)}, u32[]{:S(2)}) %collective-permute-start.1) | collective-permute-done | bytes 131104 | tf_op jit(solution)/shard_map/ppermute | solution.py:232
  19.3 0.0 copy-done
  19.3 0.7 %copy-done.1 = bf16[2,16,2048]{2,1,0:T(8,128)(2,1)} copy-done((bf16[2,16,2048]{2,1,0:T(8,128)(2,1)}, bf16[2,16,2048]{2,1,0:T(8,128)(2,1)S(1)}, u32[]{:S(2)}) %copy-start.1) | copy-done | bytes 131096
  19.9 4.7 %weighted_sums.1 = bf16[4,2,128,256]{3,2,1,0:T(8,128)(2,1)} custom-call(s32[2,2,2]{2,1,0:T(2,128)} %index_hbm.1, s32[2,2]{1,0:T(2,128)} %bounds_hbm.3, f32[16,21]{1,0:T(8,128)} %bank_hbm.1, bf16[2,16,2048]{2,1,0:T(8,128)(2,1)} %copy-done, bf16[2,16,2048]{2,1,0:T(8,128)(2,1)} %copy-done.1, bf16[2,128,2048]{2,1,0:T(8,128)(2,1)} %pixels_hbm.3, ...), custom_call_target="tpu_custom_call" | custom-call | tf_op jit(solution)/shard_map/weighted_sums/pallas_call | solution.py:235
  24.6 0.0 all-to-all-done.1
  24.6 4.2 %all-to-all-start = ((bf16[4,2,128,256]{3,2,1,0:T(8,128)(2,1)}), bf16[4,2,128,256]{3,2,1,0:T(8,128)(2,1)S(1)}, u32[]{:S(2)}, u32[]{:S(2)}) async-start(bf16[4,2,128,256]{3,2,1,0:T(8,128)(2,1)} %weighted_sums.1), calls=%async_computation | async-start | bytes 1048576 | tf_op jit(solution)/shard_map/all_to_all | solution.py:210
  28.8 0.1 convert_reduce_fusion
  28.9 7.5 %collective-permute-start.3 = (bf16[128,256]{1,0:T(8,128)(2,1)S(1)}, bf16[128,256]{1,0:T(8,128)(2,1)S(1)}, u32[]{:S(2)}, u32[]{:S(2)}) collective-permute-start(bf16[128,256]{1,0:T(8,128)(2,1)S(1)} %fusion.2), channel_id=1, source_target_pairs={{0,16},{4,20},{8,24},{12,28},{16,0},{20,4},{24,8},{28,12},{1,17},{... | collective-permute-start | bytes 196616 | tf_op jit(solution)/shard_map/ppermute | solution.py:234
  36.4 1.8 %all-to-all-done = bf16[4,2,128,256]{3,2,1,0:T(8,128)(2,1)S(1)} async-done(((bf16[4,2,128,256]{3,2,1,0:T(8,128)(2,1)}), bf16[4,2,128,256]{3,2,1,0:T(8,128)(2,1)S(1)}, u32[]{:S(2)}, u32[]{:S(2)}) %all-to-all-start) | async-done | bytes 524320 | tf_op jit(solution)/shard_map/all_to_all | solution.py:210
  38.2 0.1 convert_reduce_fusion.1
  38.3 5.6 %collective-permute-start.2 = (bf16[128,256]{1,0:T(8,128)(2,1)S(1)}, bf16[128,256]{1,0:T(8,128)(2,1)S(1)}, u32[]{:S(2)}, u32[]{:S(2)}) collective-permute-start(bf16[128,256]{1,0:T(8,128)(2,1)S(1)} %fusion.1), channel_id=1, source_target_pairs={{0,16},{4,20},{8,24},{12,28},{16,0},{20,4},{24,8},{28,12},{1,17},{... | collective-permute-start | bytes 196616 | tf_op jit(solution)/shard_map/ppermute | solution.py:263
  43.9 0.0 collective-permute-done.3
  43.9 4.4 %collective-permute-done.2 = bf16[128,256]{1,0:T(8,128)(2,1)S(1)} collective-permute-done((bf16[128,256]{1,0:T(8,128)(2,1)S(1)}, bf16[128,256]{1,0:T(8,128)(2,1)S(1)}, u32[]{:S(2)}, u32[]{:S(2)}) %collective-permute-start.2) | collective-permute-done | bytes 65568 | tf_op jit(solution)/shard_map/ppermute | solution.py:263
  48.3 0.7 %fusion = (f32[128,256]{1,0:T(8,128)}, f32[128,256]{1,0:T(8,128)}) fusion(bf16[128,256]{1,0:T(8,128)(2,1)S(1)} %collective-permute-done.2, f32[2,128,256]{2,1,0:T(8,128)S(1)} %convert_reduce_fusion.1, pred[]{:T(512)S(6)} %eq.2, bf16[128,256]{1,0:T(8,128)(2,1)S(1)} %collective-permute-done.3, f32[2,128,256]{2,1,0:T(8,128)S(1)} %convert_reduce_fusion), kind=kLoop, calls=%fused_computation.4 | loop fusion | flops 262144 | bytes 917505 | tf_op jit(solution)/shard_map/div | solution.py:265
  (3 shorter events, 0.0 us)
Async XLA Ops:
  2.8 5.0 %copy-start.3 = (bf16[2,16,2048]{2,1,0:T(8,128)(2,1)S(1)}, bf16[2,16,2048]{2,1,0:T(8,128)(2,1)}, u32[]{:S(2)}) copy-start(bf16[2,16,2048]{2,1,0:T(8,128)(2,1)} %get-tuple-element.5) | copy-start | bytes 393220
  2.8 9.8 %copy-start.2 = (bf16[2,16,2048]{2,1,0:T(8,128)(2,1)S(1)}, bf16[2,16,2048]{2,1,0:T(8,128)(2,1)}, u32[]{:S(2)}) copy-start(bf16[2,16,2048]{2,1,0:T(8,128)(2,1)} %get-tuple-element.6) | copy-start | bytes 393220
  2.8 21.7 %all-to-all-start.1 = ((bf16[4,2,128,256]{3,2,1,0:T(8,128)(2,1)}), bf16[4,2,128,256]{3,2,1,0:T(8,128)(2,1)S(1)}, u32[]{:S(2)}, u32[]{:S(2)}) async-start(bf16[4,2,128,256]{3,2,1,0:T(8,128)(2,1)} %get-tuple-element.7), calls=%async_computation.1 | async-start | bytes 1048576 | tf_op jit(solution)/shard_map/all_to_all | solution.py:210
  7.8 8.8 %collective-permute-start = (bf16[2,16,2048]{2,1,0:T(8,128)(2,1)S(1)}, bf16[2,16,2048]{2,1,0:T(8,128)(2,1)S(1)}, u32[]{:S(2)}, u32[]{:S(2)}) collective-permute-start(bf16[2,16,2048]{2,1,0:T(8,128)(2,1)S(1)} %copy-done.3), channel_id=1, source_target_pairs={{0,32},{32,64},{64,96},{96,128},{128,160},{160,192},{192,224},{224... | collective-permute-start | bytes 393224 | tf_op jit(solution)/shard_map/ppermute | solution.py:231
  12.7 6.6 %collective-permute-start.1 = (bf16[2,16,2048]{2,1,0:T(8,128)(2,1)S(1)}, bf16[2,16,2048]{2,1,0:T(8,128)(2,1)S(1)}, u32[]{:S(2)}, u32[]{:S(2)}) collective-permute-start(bf16[2,16,2048]{2,1,0:T(8,128)(2,1)S(1)} %copy-done.2), channel_id=1, source_target_pairs={{32,0},{64,32},{96,64},{128,96},{160,128},{192,160},{224,192},{256... | collective-permute-start | bytes 393224 | tf_op jit(solution)/shard_map/ppermute | solution.py:232
  16.6 2.7 %copy-start = (bf16[2,16,2048]{2,1,0:T(8,128)(2,1)}, bf16[2,16,2048]{2,1,0:T(8,128)(2,1)S(1)}, u32[]{:S(2)}) copy-start(bf16[2,16,2048]{2,1,0:T(8,128)(2,1)S(1)} %collective-permute-done.above_hbm) | copy-start | bytes 393220
  19.3 0.7 %copy-start.1 = (bf16[2,16,2048]{2,1,0:T(8,128)(2,1)}, bf16[2,16,2048]{2,1,0:T(8,128)(2,1)S(1)}, u32[]{:S(2)}) copy-start(bf16[2,16,2048]{2,1,0:T(8,128)(2,1)S(1)} %collective-permute-done.1.below_hbm) | copy-start | bytes 393220
  24.6 13.6 %all-to-all-start = ((bf16[4,2,128,256]{3,2,1,0:T(8,128)(2,1)}), bf16[4,2,128,256]{3,2,1,0:T(8,128)(2,1)S(1)}, u32[]{:S(2)}, u32[]{:S(2)}) async-start(bf16[4,2,128,256]{3,2,1,0:T(8,128)(2,1)} %weighted_sums.1), calls=%async_computation | async-start | bytes 1048576 | tf_op jit(solution)/shard_map/all_to_all | solution.py:210
  28.9 15.0 %collective-permute-start.3 = (bf16[128,256]{1,0:T(8,128)(2,1)S(1)}, bf16[128,256]{1,0:T(8,128)(2,1)S(1)}, u32[]{:S(2)}, u32[]{:S(2)}) collective-permute-start(bf16[128,256]{1,0:T(8,128)(2,1)S(1)} %fusion.2), channel_id=1, source_target_pairs={{0,16},{4,20},{8,24},{12,28},{16,0},{20,4},{24,8},{28,12},{1,17},{... | collective-permute-start | bytes 196616 | tf_op jit(solution)/shard_map/ppermute | solution.py:234
  38.3 10.0 %collective-permute-start.2 = (bf16[128,256]{1,0:T(8,128)(2,1)S(1)}, bf16[128,256]{1,0:T(8,128)(2,1)S(1)}, u32[]{:S(2)}, u32[]{:S(2)}) collective-permute-start(bf16[128,256]{1,0:T(8,128)(2,1)S(1)} %fusion.1), channel_id=1, source_target_pairs={{0,16},{4,20},{8,24},{12,28},{16,0},{20,4},{24,8},{28,12},{1,17},{... | collective-permute-start | bytes 196616 | tf_op jit(solution)/shard_map/ppermute | solution.py:263

commit v3 on v0

v3 whole, which is shorter than its diff:
```python
import jax
import jax.numpy as jnp
from jax import lax
from jax.experimental import pallas as pl
from jax.experimental.pallas import tpu as pltpu
from jax.sharding import PartitionSpec as P

UNIT = 128
HALF = 10
TAPS = 21
NCOMP = 2
LANES = 128
EDGE = 16
FAR = 2
GROUP = 4
INNER = UNIT - 2 * EDGE
TRANSPOSED = (((1,), (1,)), ((), ()))


def toeplitz(base, rows, shift):
    width = base.shape[1]
    if shift:
        base = pltpu.roll(base, shift % width, 1)
    return pltpu.roll(jnp.broadcast_to(base, (rows, width)), 0, 1, stride=1, stride_axis=0)


def matrices(index_ref, exp, taps_ref, row_ref, own_ref, edge_ref):
    lane = lax.broadcasted_iota(jnp.int32, (EDGE, LANES), 1)
    edge_top = jnp.zeros((EDGE, LANES), jnp.float32)
    edge_bottom = jnp.zeros((EDGE, LANES), jnp.float32)
    for comp in range(NCOMP):
        base = taps_ref[pl.ds(index_ref[exp, comp, 0], 1), :]
        row_ref[exp, comp * LANES : (comp + 1) * LANES, :] = toeplitz(base, LANES, 0).astype(jnp.bfloat16)
        base = taps_ref[pl.ds(index_ref[exp, comp, 1], 1), :] * (1.0 / NCOMP)
        wide = toeplitz(base, UNIT, -HALF)
        own_ref[exp, :, comp * UNIT : (comp + 1) * UNIT] = wide[:, :UNIT].astype(jnp.bfloat16)
        short = base[:, :LANES]
        first = comp * EDGE
        top = toeplitz(short, EDGE, first + EDGE - HALF)
        edge_top = jnp.where((lane >= first) & (lane < first + EDGE), top, edge_top)
        first = (NCOMP + comp) * EDGE
        bottom = toeplitz(short, EDGE, first - EDGE - HALF)
        edge_bottom = jnp.where((lane >= first) & (lane < first + EDGE), bottom, edge_bottom)
    edge_ref[exp, :EDGE, :] = edge_top.astype(jnp.bfloat16)
    edge_ref[exp, EDGE:, :] = edge_bottom.astype(jnp.bfloat16)


def mask(bounds_ref, exp, unit):
    return jnp.where((unit >= bounds_ref[exp, 0]) & (unit < bounds_ref[exp, 1]), 1.0, 0.0)


def fill_window(window_ref, exp, pixels):
    rows, width = pixels.shape
    moved = pltpu.roll(pixels, HALF, 1)
    lane = lax.broadcasted_iota(jnp.int32, (rows, LANES), 1)
    head = moved[:, :LANES]
    window_ref[exp, :, :LANES] = jnp.where(lane < HALF, 0.0, head).astype(jnp.bfloat16)
    window_ref[exp, :, LANES:width] = moved[:, LANES:].astype(jnp.bfloat16)
    window_ref[exp, :, width:] = jnp.where(lane < HALF, head, 0.0).astype(jnp.bfloat16)


def row_filter(window_ref, exp, matrix, start, count):
    stacked = jnp.concatenate(
        [window_ref[exp, :, block * LANES : (block + 2) * LANES] for block in range(start, start + count)], axis=0
    )
    return lax.dot_general(stacked, matrix, TRANSPOSED, preferred_element_type=jnp.float32).astype(jnp.bfloat16)


def start_all(pairs, sems):
    copies = [pltpu.make_async_copy(source, target, sems.at[i]) for i, (source, target) in enumerate(pairs)]
    for copy in copies:
        copy.start()
    return copies


def wait_all(copies):
    for copy in copies:
        copy.wait()


def own_sums(
    index_hbm, bounds_hbm, bank_hbm, pixels_hbm, variance_hbm,
    out_hbm, core_hbm, link_hbm, strips_hbm, row_hbm, edge_hbm,
    index_ref, bounds_ref, bank_ref, pixels_ref, variance_ref, out_ref, strips_ref, row_ref, edge_ref,
    taps_ref, own_ref, window_ref, across_ref, in_sems, out_sems,
):
    unit = lax.axis_index("patch")
    odd = lax.rem(unit, 2)
    exp_count, rows, width = pixels_ref.shape
    near, _, share = out_ref.shape
    sources = [(index_hbm, index_ref), (bank_hbm, bank_ref), (bounds_hbm, bounds_ref)]
    sources += [(pixels_hbm.at[e], pixels_ref.at[e]) for e in range(exp_count)]
    sources += [(variance_hbm.at[e], variance_ref.at[e]) for e in range(exp_count)]
    arrivals = start_all(sources, in_sems)
    wait_all(arrivals[:3])
    bank = bank_ref[...]
    bank = (bank / jnp.sum(bank, axis=1, keepdims=True)).astype(jnp.bfloat16).astype(jnp.float32)
    taps_ref[...] = jnp.concatenate([bank, jnp.zeros((bank.shape[0], 2 * LANES - TAPS), jnp.float32)], axis=1)
    for exp in range(exp_count):
        matrices(index_ref, exp, taps_ref, row_ref, own_ref, edge_ref)
    for exp in range(exp_count):
        arrivals[3 + exp].wait()
        fill_window(window_ref, exp, pixels_ref[exp].astype(jnp.float32))
        for start in range(0, width // LANES, GROUP):
            filtered = row_filter(window_ref, exp, row_ref[exp], start, GROUP)
            for block in range(GROUP):
                at = slice((start + block) * LANES, (start + block + 1) * LANES)
                for comp in range(NCOMP):
                    across_ref[exp, comp * UNIT : (comp + 1) * UNIT, at] = filtered[
                        block * UNIT : (block + 1) * UNIT, comp * LANES : (comp + 1) * LANES
                    ]
    to_core = pl.multiple_of((1 - odd) * (rows - EDGE), EDGE)
    to_link = pl.multiple_of(odd * (rows - EDGE), EDGE)
    leaves = start_all(
        [
            (pixels_ref.at[:, pl.ds(to_core, EDGE)], core_hbm),
            (pixels_ref.at[:, pl.ds(to_link, EDGE)], link_hbm),
            (row_ref, row_hbm),
            (edge_ref, edge_hbm),
        ],
        out_sems,
    )
    wait_all(arrivals[3 + exp_count :])
    masks = [mask(bounds_ref, exp, unit) for exp in range(exp_count)]
    for part in range(width // share):
        far, x = divmod(part, near)
        at = slice(part * share, (part + 1) * share)
        numer = jnp.zeros((rows, share), jnp.float32)
        denom = jnp.zeros((rows, share), jnp.float32)
        for exp in range(exp_count):
            weights = variance_ref[exp, :, at].astype(jnp.float32) * masks[exp]
            numer += weights * jnp.dot(own_ref[exp], across_ref[exp, :, at], preferred_element_type=jnp.float32)
            denom += weights
        row = far * (INNER + UNIT)
        out_ref[x, row : row + INNER, :] = numer[EDGE : UNIT - EDGE].astype(jnp.bfloat16)
        out_ref[x, row + INNER : row + INNER + UNIT, :] = denom.astype(jnp.bfloat16)
        strips_ref[:EDGE, at] = numer[:EDGE]
        strips_ref[EDGE:, at] = numer[UNIT - EDGE :]
        lines = pl.ds(row, INNER + UNIT)
        leaves.append(pltpu.make_async_copy(out_ref.at[x, lines], out_hbm.at[x, lines], out_sems.at[len(leaves)]))
        leaves[-1].start()
    leaves.append(pltpu.make_async_copy(strips_ref, strips_hbm, out_sems.at[len(leaves)]))
    leaves[-1].start()
    wait_all(leaves)


def strip_sums(
    bounds_ref, place_ref, core_ref, link_ref, top_ref, bottom_ref, strips_ref, row_ref, edge_ref,
    keep_ref, give_ref, window_ref, across_ref,
):
    unit, far = place_ref[0], place_ref[1]
    odd = lax.rem(unit, 2) == 1
    exp_count, _, width = core_ref.shape
    total = strips_ref[...]
    for exp in range(exp_count):
        core, link = core_ref[exp].astype(jnp.float32), link_ref[exp].astype(jnp.float32)
        above = jnp.where(odd, core, link) * mask(bounds_ref, exp, unit - 1)
        below = jnp.where(odd, link, core) * mask(bounds_ref, exp, unit + 1)
        fill_window(window_ref, 0, jnp.concatenate([above, below], axis=0))
        blocks = width // LANES
        filtered = row_filter(window_ref, 0, row_ref[exp], 0, blocks)
        for block in range(blocks):
            at = slice(block * LANES, (block + 1) * LANES)
            for comp in range(NCOMP):
                mine = filtered[block * 2 * EDGE : (block + 1) * 2 * EDGE, comp * LANES : (comp + 1) * LANES]
                across_ref[comp * EDGE : (comp + 1) * EDGE, at] = mine[:EDGE]
                first = (NCOMP + comp) * EDGE
                across_ref[first : first + EDGE, at] = mine[EDGE:]
        smoothed = jnp.dot(
            edge_ref[exp, :, : 2 * NCOMP * EDGE], across_ref[...], preferred_element_type=jnp.float32
        )
        weights = jnp.concatenate([top_ref[exp], bottom_ref[exp]], axis=0).astype(jnp.float32)
        total = total + weights * mask(bounds_ref, exp, unit) * smoothed
    near, _, share = keep_ref.shape
    for x in range(near):
        first = total[:, x * share : (x + 1) * share]
        second = total[:, (near + x) * share : (near + x + 1) * share]
        keep_ref[x] = jnp.where(far == 0, first, second)
        give_ref[x] = jnp.where(far == 0, second, first).astype(give_ref.dtype)


def whole(shape):
    return pl.BlockSpec(shape, lambda *_: (0,) * len(shape))


def shards(exposures, inv_variance, strip_bounds, kernel_index, basis_bank):
    exp_count, row_count, width = exposures.shape
    patches, parts = lax.axis_size("patch"), lax.axis_size("epoch")
    near = parts // FAR
    share = width // parts
    f32, bf16 = jnp.float32, jnp.bfloat16
    hbm = pl.BlockSpec(memory_space=pl.ANY)
    far = jnp.where(lax.axis_index("epoch") >= near, 1, 0)
    groups = [[y * near + x for x in range(near)] for y in range(FAR)]
    swap = [(at, (at + near) % parts) for at in range(parts)]
    lines = INNER + row_count

    def shape(*dims, dtype=bf16):
        return jax.ShapeDtypeStruct(dims, dtype)

    def vmem(struct):
        return pltpu.VMEM(struct.shape, struct.dtype)

    strip = shape(exp_count, EDGE, width)
    sends = shape(near, FAR * lines, share)
    edge_rows = shape(2 * EDGE, width, dtype=f32)
    row_mat = shape(exp_count, NCOMP * LANES, 2 * LANES)
    edge_mat = shape(exp_count, 2 * EDGE, LANES)
    sums, to_core, to_link, strips, row_mats, edge_mats = pl.pallas_call(
        own_sums,
        out_shape=(sends, strip, strip, edge_rows, row_mat, edge_mat),
        in_specs=[hbm] * 5,
        out_specs=(hbm,) * 6,
        scratch_shapes=[
            pltpu.SMEM(kernel_index.shape, jnp.int32),
            pltpu.SMEM(strip_bounds.shape, jnp.int32),
            vmem(basis_bank),
            vmem(exposures),
            vmem(inv_variance),
            vmem(sends),
            vmem(edge_rows),
            vmem(row_mat),
            vmem(edge_mat),
            pltpu.VMEM((basis_bank.shape[0], 2 * LANES), f32),
            pltpu.VMEM((exp_count, UNIT, NCOMP * UNIT), bf16),
            pltpu.VMEM((exp_count, UNIT, width + LANES), bf16),
            pltpu.VMEM((exp_count, NCOMP * UNIT, width), bf16),
            pltpu.SemaphoreType.DMA((3 + 2 * exp_count,)),
            pltpu.SemaphoreType.DMA((5 + parts,)),
        ],
        name="own_sums",
    )(kernel_index, strip_bounds, basis_bank, exposures, inv_variance)

    received = lax.all_to_all(sums, "epoch", 0, 0, tiled=True, axis_index_groups=groups)

    from_core = lax.ppermute(to_core, "patch", [(at, at ^ 1) for at in range(patches)])
    from_link = lax.ppermute(to_link, "patch", [(at, ((at + 1) ^ 1) - 1) for at in range(1, patches - 1)])
    smem = pl.BlockSpec(memory_space=pltpu.SMEM)
    place = jnp.stack([lax.axis_index("patch"), far]).astype(jnp.int32)
    strip_keep, strip_give = pl.pallas_call(
        strip_sums,
        out_shape=(shape(near, 2 * EDGE, share, dtype=f32), shape(near, 2 * EDGE, share)),
        grid=(1,),
        in_specs=[
            smem,
            smem,
            whole(strip.shape),
            whole(strip.shape),
            pl.BlockSpec(strip.shape, lambda i: (0, 0, 0)),
            pl.BlockSpec(strip.shape, lambda i: (0, row_count // EDGE - 1, 0)),
            whole(strips.shape),
            whole(row_mats.shape),
            whole(edge_mats.shape),
        ],
        out_specs=(whole((near, 2 * EDGE, share)), whole((near, 2 * EDGE, share))),
        scratch_shapes=[
            pltpu.VMEM((1, 2 * EDGE, width + LANES), bf16),
            pltpu.VMEM((2 * NCOMP * EDGE, width), bf16),
        ],
        name="strip_sums",
    )(strip_bounds, place, from_core, from_link, inv_variance, inv_variance, strips, row_mats, edge_mats)

    received, strip_give = lax.optimization_barrier((received, strip_give))
    received = received.reshape(near, FAR, lines, share)

    def half(at):
        return jnp.sum(lax.dynamic_index_in_dim(received, at, 1, keepdims=False).astype(f32), axis=0)

    keep, give = half(far), half(1 - far).astype(bf16)
    inner = keep + lax.ppermute(give, "epoch", swap).astype(f32)
    strip_sum = (strip_keep + lax.ppermute(strip_give, "epoch", swap).astype(f32)).astype(bf16)

    strip_parts = lax.all_to_all(strip_sum, "epoch", 0, 0, tiled=True, axis_index_groups=groups)
    edges = jnp.sum(strip_parts.astype(f32), axis=0)

    numer = jnp.concatenate([edges[:EDGE], inner[:INNER], edges[EDGE:]], axis=0)
    denom = inner[INNER:]
    return numer / jnp.maximum(denom, 1.0), denom


def solution(mesh):
    return jax.shard_map(
        shards,
        mesh=mesh,
        in_specs=(
            P(("band", "epoch"), "patch", None),
            P(("band", "epoch"), "patch", None),
            P(("band", "epoch"), None),
            P(("band", "epoch"), None, None),
            P(),
        ),
        out_specs=(P(("band", "patch"), "epoch"), P(("band", "patch"), "epoch")),
        check_vma=False,
    )
```

time: 198 us -> 47.2 us (0.24); the launches traced: 195 us -> 46.8 us
  waiting for transfers between devices: 139 us -> 8.41 us
  starting transfers between devices: 10.1 us -> 28.1 us
  between operations: 14.4 us -> 0.77 us
  other arithmetic: 14.1 us -> 2.19 us
  local copies, waits for them, and re-layouts: 12.4 us -> 0.69 us
  Pallas kernels: 0 us -> 6.67 us
  matrix products: 5.07 us -> 0 us
    psum x1 -> x0, waiting for transfers between devices: 139 us -> none  [shards(): numer_full, denom_full = lax.psum((numer, denom), 'epoch')]
    all_to_all x0 -> x2, starting transfers between devices: none -> 9.38 us  [the longest x1 4.99 us: shards(): lax.all_to_all(sums, 'epoch', 0, 0, tiled=True, axis_index_groups=groups)]
    ppermute x2 -> x4, starting transfers between devices: 10.1 us -> 18.7 us  [the longest x1 7.47 us: shards(): lax.ppermute(to_core, 'patch', [(at, at ^ 1) for at in range(patches)])]
    reduce_sum x2 -> x3, other arithmetic: 8.03 us -> 0.15 us  [the longest x2 0.13 us: half(): jnp.sum(lax.dynamic_index_in_dim(received, at, 1, keepdims=False).astype(...]
    pallas_call x0 -> x2, Pallas kernels: none -> 6.67 us  [the longest x1 3.82 us: shards(): pl.pallas_call(own_sums, out_shape=(sends, strip, strip, edge_rows, row_m...]
    unnamed x30 -> x10, local copies, waits for them, and re-layouts: 5.93 us -> 0.67 us
    dot_general x9 -> x0, matrix products: 5.07 us -> none  [the longest x4 2.55 us: horizontal(): jnp.einsum('rbi,ij->rbj', window, matrix, preferred_element_type=jnp.floa...]
    ppermute x2 -> x4, waiting for transfers between devices: 0.01 us -> 4.68 us  [the longest x1 3.97 us: shards(): lax.ppermute(to_link, 'patch', [(at, (at + 1 ^ 1) - 1) for at in range(1,...]
  transfers between devices with their start and end apart: 3 -> 6, of which waited for: 1 -> 3; matrix products, arithmetic and copies ran while one was open for 5% -> 3% of each run, Pallas kernels for 0% -> 6%
where the time goes in v3:
time: 47.2 us; the launch traced here: 46.8 us
  starting transfers between devices  28.1 us (60%)
  waiting for transfers between devices  8.41 us (18%)
  Pallas kernels  6.67 us (14%)
  other arithmetic  2.19 us (5%)
  between operations  0.77 us (2%)
  local copies, waits for them, and re-layouts  0.69 us (1%)
    ppermute x1, starting transfers between devices, shards(): lax.ppermute(to_core, 'patch', [(at, at ^ 1) for at in range(patches)])  7.47 us
    ppermute x1, starting transfers between devices, shards(): inner = keep + lax.ppermute(give, 'epoch', swap).astype(f32)  6.23 us
    all_to_all x1, starting transfers between devices, shards(): lax.all_to_all(sums, 'epoch', 0, 0, tiled=True, axis_index_groups=groups)  4.99 us
    all_to_all x1, starting transfers between devices, shards(): lax.all_to_all(strip_sum, 'epoch', 0, 0, tiled=True, axis_index_groups=gr...  4.39 us
    ppermute x1, waiting for transfers between devices, shards(): lax.ppermute(to_link, 'patch', [(at, (at + 1 ^ 1) - 1) for at in range(1,...  3.97 us
    pallas_call x1, Pallas kernels, shards(): pl.pallas_call(own_sums, out_shape=(sends, strip, strip, edge_rows, row_m...  3.82 us
    all_to_all x1, waiting for transfers between devices, shards(): lax.all_to_all(strip_sum, 'epoch', 0, 0, tiled=True, axis_index_groups=gr...  3.73 us
    ppermute x1, starting transfers between devices, shards(): lax.ppermute(strip_give, 'epoch', swap).astype(f32)  3.08 us
  transfers between devices with their start and end apart: 6, of which 3 were waited for; matrix products, arithmetic and copies ran while one was open for 3% of the time, Pallas kernels for 6%

profile of v3, /device:TPU:1, one launch (start us, length us, event | category | flops | bytes accessed | tf_op | source)
XLA Modules:
  0.0 46.8 jit_solution(9837961941560170846)
XLA Ops:
  0.6 3.8 %own_sums.1 = (bf16[4,448,256]{2,1,0:T(8,128)(2,1)}, bf16[2,16,2048]{2,1,0:T(8,128)(2,1)}, bf16[2,16,2048]{2,1,0:T(8,128)(2,1)}, f32[32,2048]{1,0:T(8,128)}, bf1...) custom-call(s32[2,2,2]{2,1,0:T(2,128)} %index_hbm.1, s32[2,2]{1,0:T(2,128)} %bounds_ref.1, f32[16,21]{1,0:T(8,128)} %bank_hbm.1, ...), custom_call_target="tpu_custom_call" | custom-call | tf_op jit(solution)/shard_map/own_sums/pallas_call | solution.py:209
  4.5 0.0 copy-start.4
  4.5 0.0 copy-start.3
  4.5 5.0 %all-to-all-start = ((bf16[4,448,256]{2,1,0:T(8,128)(2,1)}), bf16[4,448,256]{2,1,0:T(8,128)(2,1)S(1)}, u32[]{:S(2)}, u32[]{:S(2)}) async-start(bf16[4,448,256]{2,1,0:T(8,128)(2,1)} %get-tuple-element.18), calls=%async_computation | async-start | bytes 1835008 | tf_op jit(solution)/shard_map/all_to_all | solution.py:234
  9.5 0.0 copy-done.4
  9.5 7.5 %collective-permute-start = (bf16[2,16,2048]{2,1,0:T(8,128)(2,1)S(1)}, bf16[2,16,2048]{2,1,0:T(8,128)(2,1)S(1)}, u32[]{:S(2)}, u32[]{:S(2)}) collective-permute-start(bf16[2,16,2048]{2,1,0:T(8,128)(2,1)S(1)} %copy-done.4), channel_id=1, source_target_pairs={{0,32},{32,0},{64,96},{96,64},{128,160},{160,128},{192,224},{224,1... | collective-permute-start | bytes 393224 | tf_op jit(solution)/shard_map/ppermute | solution.py:236
  17.0 1.9 %collective-permute-start.1 = (bf16[2,16,2048]{2,1,0:T(8,128)(2,1)S(1)}, bf16[2,16,2048]{2,1,0:T(8,128)(2,1)S(1)}, u32[]{:S(2)}, u32[]{:S(2)}) collective-permute-start(bf16[2,16,2048]{2,1,0:T(8,128)(2,1)S(1)} %copy-done.3), channel_id=1, source_target_pairs={{32,64},{64,32},{96,128},{128,96},{160,192},{192,160},{224,256},{2... | collective-permute-start | bytes 393224 | tf_op jit(solution)/shard_map/ppermute | solution.py:237
  18.9 0.7 %pad_add_fusion.place_ref = s32[2]{0:T(128)} fusion(s32[1]{0:T(128)} %bitcast.1, s32[1]{0:T(128)} %bitcast), kind=kLoop, calls=%fused_computation.6 | loop fusion | flops 2 | bytes 16 | tf_op jit(solution)/shard_map/stack | solution.py:239
  19.6 0.0 collective-permute-done.core_ref
  19.6 4.0 %collective-permute-done.1.link_ref = bf16[2,16,2048]{2,1,0:T(8,128)(2,1)S(1)} collective-permute-done((bf16[2,16,2048]{2,1,0:T(8,128)(2,1)S(1)}, bf16[2,16,2048]{2,1,0:T(8,128)(2,1)S(1)}, u32[]{:S(2)}, u32[]{:S(2)}) %collective-permute-start.1) | collective-permute-done | bytes 131104 | tf_op jit(solution)/shard_map/ppermute | solution.py:237
  23.5 0.0 copy-done
  23.5 0.7 %copy-done.1 = bf16[2,16,2048]{2,1,0:T(8,128)(2,1)} copy-done((bf16[2,16,2048]{2,1,0:T(8,128)(2,1)}, bf16[2,16,2048]{2,1,0:T(8,128)(2,1)S(1)}, u32[]{:S(2)}) %copy-start.1) | copy-done | bytes 131096
  24.2 2.8 %strip_sums.1 = (f32[4,32,256]{2,1,0:T(8,128)}, bf16[4,32,256]{2,1,0:T(8,128)(2,1)}) custom-call(s32[2,2]{1,0:T(2,128)} %bounds_ref.1, s32[2]{0:T(128)} %pad_add_fusion.place_ref, bf16[2,16,2048]{2,1,0:T(8,128)(2,1)} %copy-done, bf16[2,16,2048]{2,1,0:T(8,128)(2,1)} %copy-done.1, bf16[2,128,2048]{2,1,0:T(8,128)(2,1)} %bottom_ref.1, ...), custom_call_target="tpu_custom_call" | custom-call | tf_op jit(solution)/shard_map/strip_sums/pallas_call | solution.py:240
  27.0 0.0 all-to-all-done
  27.0 3.1 %collective-permute-start.2 = (bf16[4,32,256]{2,1,0:T(8,128)(2,1)}, bf16[4,32,256]{2,1,0:T(8,128)(2,1)S(1)}, u32[]{:S(2)}, u32[]{:S(2)}) collective-permute-start(bf16[4,32,256]{2,1,0:T(8,128)(2,1)} %get-tuple-element.20), channel_id=1, source_target_pairs={{0,16},{4,20},{8,24},{12,28},{16,0},{20,4},{24,8},{28,12},{1,17},{... | collective-permute-start | bytes 196616 | tf_op jit(solution)/shard_map/ppermute | solution.py:271
  30.1 0.1 dynamic-slice_reduce_fusion
  30.2 6.2 %collective-permute-start.3 = (bf16[224,256]{1,0:T(8,128)(2,1)S(1)}, bf16[224,256]{1,0:T(8,128)(2,1)S(1)}, u32[]{:S(2)}, u32[]{:S(2)}) collective-permute-start(bf16[224,256]{1,0:T(8,128)(2,1)S(1)} %dynamic-slice_reduce_fusion), channel_id=1, source_target_pairs={{0,16},{4,20},{8,24},{12,28},{16,0},{20,4},{24,8},{28,12},{1,17},{... | collective-permute-start | bytes 344072 | tf_op jit(solution)/shard_map/ppermute | solution.py:270
  36.5 0.1 convert_reduce_fusion
  36.5 0.0 collective-permute-done.2
  36.6 0.6 %add_convert_fusion = bf16[4,32,256]{2,1,0:T(8,128)(2,1)} fusion(f32[4,32,256]{2,1,0:T(8,128)S(1)} %copy-done.2, bf16[4,32,256]{2,1,0:T(8,128)(2,1)S(1)} %collective-permute-done.2), kind=kLoop, calls=%fused_computation.5 | loop fusion | flops 98304 | bytes 262144 | tf_op jit(solution)/shard_map/convert_element_type | solution.py:271
  37.2 4.4 %all-to-all-start.1 = ((bf16[4,32,256]{2,1,0:T(8,128)(2,1)}), bf16[4,32,256]{2,1,0:T(8,128)(2,1)S(1)}, u32[]{:S(2)}, u32[]{:S(2)}) async-start(bf16[4,32,256]{2,1,0:T(8,128)(2,1)} %add_convert_fusion), calls=%async_computation.1 | async-start | bytes 131072 | tf_op jit(solution)/shard_map/all_to_all | solution.py:273
  41.6 0.7 %collective-permute-done.3 = bf16[224,256]{1,0:T(8,128)(2,1)S(1)} collective-permute-done((bf16[224,256]{1,0:T(8,128)(2,1)S(1)}, bf16[224,256]{1,0:T(8,128)(2,1)S(1)}, u32[]{:S(2)}, u32[]{:S(2)}) %collective-permute-start.3) | collective-permute-done | bytes 114720 | tf_op jit(solution)/shard_map/ppermute | solution.py:270
  42.3 3.7 %all-to-all-done.1 = bf16[4,32,256]{2,1,0:T(8,128)(2,1)S(1)} async-done(((bf16[4,32,256]{2,1,0:T(8,128)(2,1)}), bf16[4,32,256]{2,1,0:T(8,128)(2,1)S(1)}, u32[]{:S(2)}, u32[]{:S(2)}) %all-to-all-start.1) | async-done | bytes 65568 | tf_op jit(solution)/shard_map/all_to_all | solution.py:273
  46.1 0.7 %maximum_divide_fusion = (f32[128,256]{1,0:T(8,128)}, f32[128,256]{1,0:T(8,128)}) fusion(f32[16,256]{1,0:T(8,128)S(1)} %get-tuple-element.25, f32[96,256]{1,0:T(8,128)S(1)} %slice.17, f32[16,256]{1,0:T(8,128)S(1)} %get-tuple-element.24, f32[224,256]{1,0:T(8,128)S(1)} %convert_add_fusion), kind=kLoop, calls=%fused_computation.3 | loop fusion | flops 131072 | bytes 524288 | tf_op jit(solution)/shard_map/div | solution.py:278
  (9 shorter events, 0.1 us)
Async XLA Ops:
  4.5 5.0 %copy-start.4 = (bf16[2,16,2048]{2,1,0:T(8,128)(2,1)S(1)}, bf16[2,16,2048]{2,1,0:T(8,128)(2,1)}, u32[]{:S(2)}) copy-start(bf16[2,16,2048]{2,1,0:T(8,128)(2,1)} %get-tuple-element.12) | copy-start | bytes 393220
  4.5 12.5 %copy-start.3 = (bf16[2,16,2048]{2,1,0:T(8,128)(2,1)S(1)}, bf16[2,16,2048]{2,1,0:T(8,128)(2,1)}, u32[]{:S(2)}) copy-start(bf16[2,16,2048]{2,1,0:T(8,128)(2,1)} %get-tuple-element.13) | copy-start | bytes 393220
  4.5 22.6 %all-to-all-start = ((bf16[4,448,256]{2,1,0:T(8,128)(2,1)}), bf16[4,448,256]{2,1,0:T(8,128)(2,1)S(1)}, u32[]{:S(2)}, u32[]{:S(2)}) async-start(bf16[4,448,256]{2,1,0:T(8,128)(2,1)} %get-tuple-element.18), calls=%async_computation | async-start | bytes 1835008 | tf_op jit(solution)/shard_map/all_to_all | solution.py:234
  9.5 10.1 %collective-permute-start = (bf16[2,16,2048]{2,1,0:T(8,128)(2,1)S(1)}, bf16[2,16,2048]{2,1,0:T(8,128)(2,1)S(1)}, u32[]{:S(2)}, u32[]{:S(2)}) collective-permute-start(bf16[2,16,2048]{2,1,0:T(8,128)(2,1)S(1)} %copy-done.4), channel_id=1, source_target_pairs={{0,32},{32,0},{64,96},{96,64},{128,160},{160,128},{192,224},{224,1... | collective-permute-start | bytes 393224 | tf_op jit(solution)/shard_map/ppermute | solution.py:236
  17.0 6.6 %collective-permute-start.1 = (bf16[2,16,2048]{2,1,0:T(8,128)(2,1)S(1)}, bf16[2,16,2048]{2,1,0:T(8,128)(2,1)S(1)}, u32[]{:S(2)}, u32[]{:S(2)}) collective-permute-start(bf16[2,16,2048]{2,1,0:T(8,128)(2,1)S(1)} %copy-done.3), channel_id=1, source_target_pairs={{32,64},{64,32},{96,128},{128,96},{160,192},{192,160},{224,256},{2... | collective-permute-start | bytes 393224 | tf_op jit(solution)/shard_map/ppermute | solution.py:237
  19.6 4.0 %copy-start = (bf16[2,16,2048]{2,1,0:T(8,128)(2,1)}, bf16[2,16,2048]{2,1,0:T(8,128)(2,1)S(1)}, u32[]{:S(2)}) copy-start(bf16[2,16,2048]{2,1,0:T(8,128)(2,1)S(1)} %collective-permute-done.core_ref) | copy-start | bytes 393220
  23.5 0.7 %copy-start.1 = (bf16[2,16,2048]{2,1,0:T(8,128)(2,1)}, bf16[2,16,2048]{2,1,0:T(8,128)(2,1)S(1)}, u32[]{:S(2)}) copy-start(bf16[2,16,2048]{2,1,0:T(8,128)(2,1)S(1)} %collective-permute-done.1.link_ref) | copy-start | bytes 393220
  27.0 9.5 %collective-permute-start.2 = (bf16[4,32,256]{2,1,0:T(8,128)(2,1)}, bf16[4,32,256]{2,1,0:T(8,128)(2,1)S(1)}, u32[]{:S(2)}, u32[]{:S(2)}) collective-permute-start(bf16[4,32,256]{2,1,0:T(8,128)(2,1)} %get-tuple-element.20), channel_id=1, source_target_pairs={{0,16},{4,20},{8,24},{12,28},{16,0},{20,4},{24,8},{28,12},{1,17},{... | collective-permute-start | bytes 196616 | tf_op jit(solution)/shard_map/ppermute | solution.py:271
  30.2 6.3 %copy-start.2 = (f32[4,32,256]{2,1,0:T(8,128)S(1)}, f32[4,32,256]{2,1,0:T(8,128)}, u32[]{:S(2)}) copy-start(f32[4,32,256]{2,1,0:T(8,128)} %get-tuple-element.17) | copy-start | bytes 393220
  30.2 12.1 %collective-permute-start.3 = (bf16[224,256]{1,0:T(8,128)(2,1)S(1)}, bf16[224,256]{1,0:T(8,128)(2,1)S(1)}, u32[]{:S(2)}, u32[]{:S(2)}) collective-permute-start(bf16[224,256]{1,0:T(8,128)(2,1)S(1)} %dynamic-slice_reduce_fusion), channel_id=1, source_target_pairs={{0,16},{4,20},{8,24},{12,28},{16,0},{20,4},{24,8},{28,12},{1,17},{... | collective-permute-start | bytes 344072 | tf_op jit(solution)/shard_map/ppermute | solution.py:270
  37.2 8.9 %all-to-all-start.1 = ((bf16[4,32,256]{2,1,0:T(8,128)(2,1)}), bf16[4,32,256]{2,1,0:T(8,128)(2,1)S(1)}, u32[]{:S(2)}, u32[]{:S(2)}) async-start(bf16[4,32,256]{2,1,0:T(8,128)(2,1)} %add_convert_fusion), calls=%async_computation.1 | async-start | bytes 131072 | tf_op jit(solution)/shard_map/all_to_all | solution.py:273

commit v4 on v3

--- a/solution.py
+++ b/solution.py
@@ -145,42 +145,55 @@
 
 
 def strip_sums(
-    bounds_ref, place_ref, core_ref, link_ref, top_ref, bottom_ref, strips_ref, row_ref, edge_ref,
-    keep_ref, give_ref, window_ref, across_ref,
+    bounds_hbm, core_ref, link_ref, variance_hbm, strips_hbm, row_hbm, edge_hbm,
+    keep_ref, give_ref,
+    bounds_ref, top_ref, bottom_ref, strips_ref, row_ref, edge_ref,
+    window_ref, across_ref, in_sems,
 ):
-    unit, far = place_ref[0], place_ref[1]
+    unit = lax.axis_index("patch")
     odd = lax.rem(unit, 2) == 1
     exp_count, _, width = core_ref.shape
+    near, _, share = keep_ref.shape
+    rows = variance_hbm.shape[1]
+    far = lax.axis_index("epoch") >= near
+    wait_all(
+        start_all(
+            [
+                (bounds_hbm, bounds_ref),
+                (row_hbm, row_ref),
+                (edge_hbm, edge_ref),
+                (strips_hbm, strips_ref),
+                (variance_hbm.at[:, pl.ds(0, EDGE)], top_ref),
+                (variance_hbm.at[:, pl.ds(rows - EDGE, EDGE)], bottom_ref),
+            ],
+            in_sems,
+        )
+    )
     total = strips_ref[...]
     for exp in range(exp_count):
         core, link = core_ref[exp].astype(jnp.float32), link_ref[exp].astype(jnp.float32)
         above = jnp.where(odd, core, link) * mask(bounds_ref, exp, unit - 1)
         below = jnp.where(odd, link, core) * mask(bounds_ref, exp, unit + 1)
-        fill_window(window_ref, 0, jnp.concatenate([above, below], axis=0))
+        fill_window(window_ref, exp, jnp.concatenate([above, below], axis=0))
         blocks = width // LANES
-        filtered = row_filter(window_ref, 0, row_ref[exp], 0, blocks)
+        filtered = row_filter(window_ref, exp, row_ref[exp], 0, blocks)
         for block in range(blocks):
             at = slice(block * LANES, (block + 1) * LANES)
             for comp in range(NCOMP):
                 mine = filtered[block * 2 * EDGE : (block + 1) * 2 * EDGE, comp * LANES : (comp + 1) * LANES]
-                across_ref[comp * EDGE : (comp + 1) * EDGE, at] = mine[:EDGE]
+                across_ref[exp, comp * EDGE : (comp + 1) * EDGE, at] = mine[:EDGE]
                 first = (NCOMP + comp) * EDGE
-                across_ref[first : first + EDGE, at] = mine[EDGE:]
+                across_ref[exp, first : first + EDGE, at] = mine[EDGE:]
         smoothed = jnp.dot(
-            edge_ref[exp, :, : 2 * NCOMP * EDGE], across_ref[...], preferred_element_type=jnp.float32
+            edge_ref[exp, :, : 2 * NCOMP * EDGE], across_ref[exp], preferred_element_type=jnp.float32
         )
         weights = jnp.concatenate([top_ref[exp], bottom_ref[exp]], axis=0).astype(jnp.float32)
         total = total + weights * mask(bounds_ref, exp, unit) * smoothed
-    near, _, share = keep_ref.shape
     for x in range(near):
         first = total[:, x * share : (x + 1) * share]
         second = total[:, (near + x) * share : (near + x + 1) * share]
-        keep_ref[x] = jnp.where(far == 0, first, second)
-        give_ref[x] = jnp.where(far == 0, second, first).astype(give_ref.dtype)
-
-
-def whole(shape):
-    return pl.BlockSpec(shape, lambda *_: (0,) * len(shape))
+        keep_ref[x] = jnp.where(far, second, first)
+        give_ref[x] = jnp.where(far, first, second).astype(give_ref.dtype)
 
 
 def shards(exposures, inv_variance, strip_bounds, kernel_index, basis_bank):
@@ -235,31 +248,26 @@
 
     from_core = lax.ppermute(to_core, "patch", [(at, at ^ 1) for at in range(patches)])
     from_link = lax.ppermute(to_link, "patch", [(at, ((at + 1) ^ 1) - 1) for at in range(1, patches - 1)])
-    smem = pl.BlockSpec(memory_space=pltpu.SMEM)
-    place = jnp.stack([lax.axis_index("patch"), far]).astype(jnp.int32)
+    keep_shape, give_shape = shape(near, 2 * EDGE, share, dtype=f32), shape(near, 2 * EDGE, share)
+    vmem_spec = pl.BlockSpec(memory_space=pltpu.VMEM)
     strip_keep, strip_give = pl.pallas_call(
         strip_sums,
-        out_shape=(shape(near, 2 * EDGE, share, dtype=f32), shape(near, 2 * EDGE, share)),
-        grid=(1,),
-        in_specs=[
-            smem,
-            smem,
-            whole(strip.shape),
-            whole(strip.shape),
-            pl.BlockSpec(strip.shape, lambda i: (0, 0, 0)),
-            pl.BlockSpec(strip.shape, lambda i: (0, row_count // EDGE - 1, 0)),
-            whole(strips.shape),
-            whole(row_mats.shape),
-            whole(edge_mats.shape),
+        out_shape=(keep_shape, give_shape),
+        in_specs=[hbm, vmem_spec, vmem_spec, hbm, hbm, hbm, hbm],
+        out_specs=(vmem_spec,) * 2,
+        scratch_shapes=[
+            pltpu.SMEM(strip_bounds.shape, jnp.int32),
+            *[vmem(strip)] * 2,
+            vmem(edge_rows),
+            vmem(row_mat),
+            vmem(edge_mat),
+            pltpu.VMEM((exp_count, 2 * EDGE, width + LANES), bf16),
+            pltpu.VMEM((exp_count, 2 * NCOMP * EDGE, width), bf16),
+            pltpu.SemaphoreType.DMA((6,)),
         ],
-        out_specs=(whole((near, 2 * EDGE, share)), whole((near, 2 * EDGE, share))),
-        scratch_shapes=[
-            pltpu.VMEM((1, 2 * EDGE, width + LANES), bf16),
-            pltpu.VMEM((2 * NCOMP * EDGE, width), bf16),
-        ],
+        compiler_params=pltpu.CompilerParams(vmem_limit_bytes=12 * 1024 * 1024),
         name="strip_sums",
-    )(strip_bounds, place, from_core, from_link, inv_variance, inv_variance, strips, row_mats, edge_mats)
-
+    )(strip_bounds, from_core, from_link, inv_variance, strips, row_mats, edge_mats)
     received, strip_give = lax.optimization_barrier((received, strip_give))
     received = received.reshape(near, FAR, lines, share)
 

time: 47.2 us -> 46.2 us (0.979)
  waiting for transfers between devices: 8.41 us -> 10.2 us
  Pallas kernels: 6.67 us -> 5.31 us
  starting transfers between devices: 28.1 us -> 27.3 us
  other arithmetic: 2.19 us -> 1.52 us
    pallas_call x1, Pallas kernels: 2.85 us -> 1.48 us  [shards(): pl.pallas_call(strip_sums, out_shape=(keep_shape, give_shape), in_specs=[...]
    ppermute x1, waiting for transfers between devices: 0.01 us -> 1.08 us  [shards(): lax.ppermute(strip_give, 'epoch', swap).astype(f32)]
    ppermute x1, starting transfers between devices: 6.23 us -> 5.21 us  [shards(): inner = keep + lax.ppermute(give, 'epoch', swap).astype(f32)]
    ppermute x1, starting transfers between devices: 3.08 us -> 3.98 us  [shards(): lax.ppermute(strip_give, 'epoch', swap).astype(f32)]
    all_to_all x1, waiting for transfers between devices: 3.73 us -> 4.52 us  [shards(): lax.all_to_all(strip_sum, 'epoch', 0, 0, tiled=True, axis_index_groups=gr...]
    ppermute x1, waiting for transfers between devices: 0.7 us -> 0.01 us  [shards(): inner = keep + lax.ppermute(give, 'epoch', swap).astype(f32)]
    ppermute x1, waiting for transfers between devices: 3.97 us -> 4.64 us  [shards(): lax.ppermute(to_link, 'patch', [(at, (at + 1 ^ 1) - 1) for at in range(1,...]
    another operation x1 -> x0, other arithmetic: 0.67 us -> none  [shards(): place = jnp.stack([lax.axis_index('patch'), far]).astype(jnp.int32)]
  transfers between devices with their start and end apart: 6 -> 6, of which waited for: 3 -> 3; matrix products, arithmetic and copies ran while one was open for 3% -> 2% of each run, Pallas kernels for 6% -> 3%
where the time goes in v4:
time: 46.2 us; the launch traced here: 45.9 us
  starting transfers between devices  27.3 us (59%)
  waiting for transfers between devices  10.2 us (22%)
  Pallas kernels  5.31 us (11%)
  other arithmetic  1.52 us (3%)
  between operations  0.8 us (2%)
  local copies, waits for them, and re-layouts  0.7 us (2%)
    ppermute x1, starting transfers between devices, shards(): lax.ppermute(to_core, 'patch', [(at, at ^ 1) for at in range(patches)])  7.46 us
    ppermute x1, starting transfers between devices, shards(): inner = keep + lax.ppermute(give, 'epoch', swap).astype(f32)  5.21 us
    all_to_all x1, starting transfers between devices, shards(): lax.all_to_all(sums, 'epoch', 0, 0, tiled=True, axis_index_groups=groups)  4.99 us
    ppermute x1, waiting for transfers between devices, shards(): lax.ppermute(to_link, 'patch', [(at, (at + 1 ^ 1) - 1) for at in range(1,...  4.64 us
    all_to_all x1, waiting for transfers between devices, shards(): lax.all_to_all(strip_sum, 'epoch', 0, 0, tiled=True, axis_index_groups=gr...  4.52 us
    ppermute x1, starting transfers between devices, shards(): lax.ppermute(strip_give, 'epoch', swap).astype(f32)  3.98 us
    pallas_call x1, Pallas kernels, shards(): pl.pallas_call(own_sums, out_shape=(sends, strip, strip, edge_rows, row_m...  3.83 us
    all_to_all x1, starting transfers between devices, shards(): lax.all_to_all(strip_sum, 'epoch', 0, 0, tiled=True, axis_index_groups=gr...  3.73 us
  transfers between devices with their start and end apart: 6, of which 3 were waited for; matrix products, arithmetic and copies ran while one was open for 2% of the time, Pallas kernels for 3%

profile of v4, /device:TPU:1, one launch (start us, length us, event | category | flops | bytes accessed | tf_op | source)
XLA Modules:
  0.0 45.9 jit_solution(3663484146269559624)
XLA Ops:
  0.6 3.8 %own_sums.1 = (bf16[4,448,256]{2,1,0:T(8,128)(2,1)}, bf16[2,16,2048]{2,1,0:T(8,128)(2,1)}, bf16[2,16,2048]{2,1,0:T(8,128)(2,1)}, f32[32,2048]{1,0:T(8,128)}, bf1...) custom-call(s32[2,2,2]{2,1,0:T(2,128)} %index_hbm.1, s32[2,2]{1,0:T(2,128)} %bounds_hbm.3, f32[16,21]{1,0:T(8,128)} %bank_hbm.1, ...), custom_call_target="tpu_custom_call" | custom-call | tf_op jit(solution)/shard_map/own_sums/pallas_call | solution.py:222
  4.5 0.0 copy-start
  4.5 0.0 copy-start.5
  4.5 0.0 copy-start.1
  4.5 0.0 copy-start.2
  4.5 0.0 copy-start.3
  4.5 5.0 %all-to-all-start = ((bf16[4,448,256]{2,1,0:T(8,128)(2,1)}), bf16[4,448,256]{2,1,0:T(8,128)(2,1)S(1)}, u32[]{:S(2)}, u32[]{:S(2)}) async-start(bf16[4,448,256]{2,1,0:T(8,128)(2,1)} %get-tuple-element.18), calls=%async_computation | async-start | bytes 1835008 | tf_op jit(solution)/shard_map/all_to_all | solution.py:247
  9.5 7.5 %collective-permute-start = (bf16[2,16,2048]{2,1,0:T(8,128)(2,1)}, bf16[2,16,2048]{2,1,0:T(8,128)(2,1)S(1)}, u32[]{:S(2)}, u32[]{:S(2)}) collective-permute-start(bf16[2,16,2048]{2,1,0:T(8,128)(2,1)} %get-tuple-element.12), channel_id=1, source_target_pairs={{0,32},{32,0},{64,96},{96,64},{128,160},{160,128},{192,224},{224,1... | collective-permute-start | bytes 393224 | tf_op jit(solution)/shard_map/ppermute | solution.py:249
  17.0 1.9 %collective-permute-start.1 = (bf16[2,16,2048]{2,1,0:T(8,128)(2,1)S(1)}, bf16[2,16,2048]{2,1,0:T(8,128)(2,1)S(1)}, u32[]{:S(2)}, u32[]{:S(2)}) collective-permute-start(bf16[2,16,2048]{2,1,0:T(8,128)(2,1)S(1)} %copy-done.5), channel_id=1, source_target_pairs={{32,64},{64,32},{96,128},{128,96},{160,192},{192,160},{224,256},{2... | collective-permute-start | bytes 393224 | tf_op jit(solution)/shard_map/ppermute | solution.py:250
  18.9 0.0 collective-permute-done.core_ref
  18.9 4.6 %collective-permute-done.1.link_ref = bf16[2,16,2048]{2,1,0:T(8,128)(2,1)S(1)} collective-permute-done((bf16[2,16,2048]{2,1,0:T(8,128)(2,1)S(1)}, bf16[2,16,2048]{2,1,0:T(8,128)(2,1)S(1)}, u32[]{:S(2)}, u32[]{:S(2)}) %collective-permute-start.1) | collective-permute-done | bytes 131104 | tf_op jit(solution)/shard_map/ppermute | solution.py:250
  23.6 0.7 %copy-done.4 = s32[2,2]{1,0:T(2,128)S(1)} copy-done((s32[2,2]{1,0:T(2,128)S(1)}, s32[2,2]{1,0:T(2,128)}, u32[]{:S(2)}) %copy-start.4) | copy-done | bytes 40
  24.2 1.5 %strip_sums.1 = (f32[4,32,256]{2,1,0:T(8,128)S(1)}, bf16[4,32,256]{2,1,0:T(8,128)(2,1)S(1)}) custom-call(s32[2,2]{1,0:T(2,128)S(1)} %copy-done.4, bf16[2,16,2048]{2,1,0:T(8,128)(2,1)S(1)} %collective-permute-done.core_ref, bf16[2,16,2048]{2,1,0:T(8,128)(2,1)S(1)} %collective-permute-done.1.link_ref, bf16[2,128,2048]{2,1,0:T(8,128)(2,1)S(1)} %copy-done, ...), custom_call_target="tpu_custom_call" | custom-call | tf_op jit(solution)/shard_map/strip_sums/pallas_call | solution.py:253
  25.7 0.0 all-to-all-done
  25.7 4.0 %collective-permute-start.2 = (bf16[4,32,256]{2,1,0:T(8,128)(2,1)S(1)}, bf16[4,32,256]{2,1,0:T(8,128)(2,1)S(1)}, u32[]{:S(2)}, u32[]{:S(2)}) collective-permute-start(bf16[4,32,256]{2,1,0:T(8,128)(2,1)S(1)} %get-tuple-element.20), channel_id=1, source_target_pairs={{0,16},{4,20},{8,24},{12,28},{16,0},{20,4},{24,8},{28,12},{1,17},{... | collective-permute-start | bytes 196616 | tf_op jit(solution)/shard_map/ppermute | solution.py:279
  29.7 0.1 dynamic-slice_reduce_fusion
  29.8 5.2 %collective-permute-start.3 = (bf16[224,256]{1,0:T(8,128)(2,1)S(1)}, bf16[224,256]{1,0:T(8,128)(2,1)S(1)}, u32[]{:S(2)}, u32[]{:S(2)}) collective-permute-start(bf16[224,256]{1,0:T(8,128)(2,1)S(1)} %dynamic-slice_reduce_fusion), channel_id=1, source_target_pairs={{0,16},{4,20},{8,24},{12,28},{16,0},{20,4},{24,8},{28,12},{1,17},{... | collective-permute-start | bytes 344072 | tf_op jit(solution)/shard_map/ppermute | solution.py:278
  35.0 0.1 convert_reduce_fusion
  35.1 1.1 %collective-permute-done.2 = bf16[4,32,256]{2,1,0:T(8,128)(2,1)S(1)} collective-permute-done((bf16[4,32,256]{2,1,0:T(8,128)(2,1)S(1)}, bf16[4,32,256]{2,1,0:T(8,128)(2,1)S(1)}, u32[]{:S(2)}, u32[]{:S(2)}) %collective-permute-start.2) | collective-permute-done | bytes 65568 | tf_op jit(solution)/shard_map/ppermute | solution.py:279
  36.2 0.6 %add_convert_fusion = bf16[4,32,256]{2,1,0:T(8,128)(2,1)} fusion(f32[4,32,256]{2,1,0:T(8,128)S(1)} %get-tuple-element.17, bf16[4,32,256]{2,1,0:T(8,128)(2,1)S(1)} %collective-permute-done.2), kind=kLoop, calls=%fused_computation.5 | loop fusion | flops 98304 | bytes 262144 | tf_op jit(solution)/shard_map/convert_element_type | solution.py:279
  36.8 3.7 %all-to-all-start.1 = ((bf16[4,32,256]{2,1,0:T(8,128)(2,1)}), bf16[4,32,256]{2,1,0:T(8,128)(2,1)S(1)}, u32[]{:S(2)}, u32[]{:S(2)}) async-start(bf16[4,32,256]{2,1,0:T(8,128)(2,1)} %add_convert_fusion), calls=%async_computation.1 | async-start | bytes 131072 | tf_op jit(solution)/shard_map/all_to_all | solution.py:281
  40.6 0.0 collective-permute-done.3
  40.6 4.5 %all-to-all-done.1 = bf16[4,32,256]{2,1,0:T(8,128)(2,1)S(1)} async-done(((bf16[4,32,256]{2,1,0:T(8,128)(2,1)}), bf16[4,32,256]{2,1,0:T(8,128)(2,1)S(1)}, u32[]{:S(2)}, u32[]{:S(2)}) %all-to-all-start.1) | async-done | bytes 65568 | tf_op jit(solution)/shard_map/all_to_all | solution.py:281
  45.2 0.7 %maximum_divide_fusion = (f32[128,256]{1,0:T(8,128)}, f32[128,256]{1,0:T(8,128)}) fusion(f32[16,256]{1,0:T(8,128)S(1)} %get-tuple-element.25, f32[96,256]{1,0:T(8,128)S(1)} %slice.17, f32[16,256]{1,0:T(8,128)S(1)} %get-tuple-element.24, f32[224,256]{1,0:T(8,128)S(1)} %convert_add_fusion), kind=kLoop, calls=%fused_computation.3 | loop fusion | flops 131072 | bytes 524288 | tf_op jit(solution)/shard_map/div | solution.py:286
  (10 shorter events, 0.1 us)
Async XLA Ops:
  4.5 19.1 %copy-start = (bf16[2,128,2048]{2,1,0:T(8,128)(2,1)S(1)}, bf16[2,128,2048]{2,1,0:T(8,128)(2,1)}, u32[]{:S(2)}) copy-start(bf16[2,128,2048]{2,1,0:T(8,128)(2,1)} %variance_hbm.3) | copy-start | bytes 3145732
  4.5 12.5 %copy-start.5 = (bf16[2,16,2048]{2,1,0:T(8,128)(2,1)S(1)}, bf16[2,16,2048]{2,1,0:T(8,128)(2,1)}, u32[]{:S(2)}) copy-start(bf16[2,16,2048]{2,1,0:T(8,128)(2,1)} %get-tuple-element.13) | copy-start | bytes 393220
  4.5 19.1 %copy-start.1 = (f32[32,2048]{1,0:T(8,128)S(1)}, f32[32,2048]{1,0:T(8,128)}, u32[]{:S(2)}) copy-start(f32[32,2048]{1,0:T(8,128)} %get-tuple-element.14.strips_hbm) | copy-start | bytes 786436
  4.5 19.1 %copy-start.2 = (bf16[2,256,256]{2,1,0:T(8,128)(2,1)S(1)}, bf16[2,256,256]{2,1,0:T(8,128)(2,1)}, u32[]{:S(2)}) copy-start(bf16[2,256,256]{2,1,0:T(8,128)(2,1)} %get-tuple-element.15.row_hbm) | copy-start | bytes 786436
  4.5 19.1 %copy-start.3 = (bf16[2,32,128]{2,1,0:T(8,128)(2,1)S(1)}, bf16[2,32,128]{2,1,0:T(8,128)(2,1)}, u32[]{:S(2)}) copy-start(bf16[2,32,128]{2,1,0:T(8,128)(2,1)} %get-tuple-element.16.edge_hbm) | copy-start | bytes 49156
  4.5 21.2 %all-to-all-start = ((bf16[4,448,256]{2,1,0:T(8,128)(2,1)}), bf16[4,448,256]{2,1,0:T(8,128)(2,1)S(1)}, u32[]{:S(2)}, u32[]{:S(2)}) async-start(bf16[4,448,256]{2,1,0:T(8,128)(2,1)} %get-tuple-element.18), calls=%async_computation | async-start | bytes 1835008 | tf_op jit(solution)/shard_map/all_to_all | solution.py:247
  9.5 9.4 %collective-permute-start = (bf16[2,16,2048]{2,1,0:T(8,128)(2,1)}, bf16[2,16,2048]{2,1,0:T(8,128)(2,1)S(1)}, u32[]{:S(2)}, u32[]{:S(2)}) collective-permute-start(bf16[2,16,2048]{2,1,0:T(8,128)(2,1)} %get-tuple-element.12), channel_id=1, source_target_pairs={{0,32},{32,0},{64,96},{96,64},{128,160},{160,128},{192,224},{224,1... | collective-permute-start | bytes 393224 | tf_op jit(solution)/shard_map/ppermute | solution.py:249
  17.0 6.6 %collective-permute-start.1 = (bf16[2,16,2048]{2,1,0:T(8,128)(2,1)S(1)}, bf16[2,16,2048]{2,1,0:T(8,128)(2,1)S(1)}, u32[]{:S(2)}, u32[]{:S(2)}) collective-permute-start(bf16[2,16,2048]{2,1,0:T(8,128)(2,1)S(1)} %copy-done.5), channel_id=1, source_target_pairs={{32,64},{64,32},{96,128},{128,96},{160,192},{192,160},{224,256},{2... | collective-permute-start | bytes 393224 | tf_op jit(solution)/shard_map/ppermute | solution.py:250
  23.6 0.7 %copy-start.4 = (s32[2,2]{1,0:T(2,128)S(1)}, s32[2,2]{1,0:T(2,128)}, u32[]{:S(2)}) copy-start(s32[2,2]{1,0:T(2,128)} %bounds_hbm.3) | copy-start | bytes 52
  25.7 10.4 %collective-permute-start.2 = (bf16[4,32,256]{2,1,0:T(8,128)(2,1)S(1)}, bf16[4,32,256]{2,1,0:T(8,128)(2,1)S(1)}, u32[]{:S(2)}, u32[]{:S(2)}) collective-permute-start(bf16[4,32,256]{2,1,0:T(8,128)(2,1)S(1)} %get-tuple-element.20), channel_id=1, source_target_pairs={{0,16},{4,20},{8,24},{12,28},{16,0},{20,4},{24,8},{28,12},{1,17},{... | collective-permute-start | bytes 196616 | tf_op jit(solution)/shard_map/ppermute | solution.py:279
  29.8 10.8 %collective-permute-start.3 = (bf16[224,256]{1,0:T(8,128)(2,1)S(1)}, bf16[224,256]{1,0:T(8,128)(2,1)S(1)}, u32[]{:S(2)}, u32[]{:S(2)}) collective-permute-start(bf16[224,256]{1,0:T(8,128)(2,1)S(1)} %dynamic-slice_reduce_fusion), channel_id=1, source_target_pairs={{0,16},{4,20},{8,24},{12,28},{16,0},{20,4},{24,8},{28,12},{1,17},{... | collective-permute-start | bytes 344072 | tf_op jit(solution)/shard_map/ppermute | solution.py:278
  36.8 8.3 %all-to-all-start.1 = ((bf16[4,32,256]{2,1,0:T(8,128)(2,1)}), bf16[4,32,256]{2,1,0:T(8,128)(2,1)S(1)}, u32[]{:S(2)}, u32[]{:S(2)}) async-start(bf16[4,32,256]{2,1,0:T(8,128)(2,1)} %add_convert_fusion), calls=%async_computation.1 | async-start | bytes 131072 | tf_op jit(solution)/shard_map/all_to_all | solution.py:281

commit v5 on v4

--- a/solution.py
+++ b/solution.py
@@ -24,7 +24,7 @@
     return pltpu.roll(jnp.broadcast_to(base, (rows, width)), 0, 1, stride=1, stride_axis=0)
 
 
-def matrices(index_ref, exp, taps_ref, row_ref, own_ref, edge_ref):
+def matrices(index_ref, exp, covers, taps_ref, row_ref, own_ref, edge_ref):
     lane = lax.broadcasted_iota(jnp.int32, (EDGE, LANES), 1)
     edge_top = jnp.zeros((EDGE, LANES), jnp.float32)
     edge_bottom = jnp.zeros((EDGE, LANES), jnp.float32)
@@ -41,8 +41,8 @@
         first = (NCOMP + comp) * EDGE
         bottom = toeplitz(short, EDGE, first - EDGE - HALF)
         edge_bottom = jnp.where((lane >= first) & (lane < first + EDGE), bottom, edge_bottom)
-    edge_ref[exp, :EDGE, :] = edge_top.astype(jnp.bfloat16)
-    edge_ref[exp, EDGE:, :] = edge_bottom.astype(jnp.bfloat16)
+    edge_ref[exp, :EDGE, :] = (edge_top * (covers[0] * covers[1])).astype(jnp.bfloat16)
+    edge_ref[exp, EDGE:, :] = (edge_bottom * (covers[1] * covers[2])).astype(jnp.bfloat16)
 
 
 def mask(bounds_ref, exp, unit):
@@ -97,7 +97,8 @@
     bank = (bank / jnp.sum(bank, axis=1, keepdims=True)).astype(jnp.bfloat16).astype(jnp.float32)
     taps_ref[...] = jnp.concatenate([bank, jnp.zeros((bank.shape[0], 2 * LANES - TAPS), jnp.float32)], axis=1)
     for exp in range(exp_count):
-        matrices(index_ref, exp, taps_ref, row_ref, own_ref, edge_ref)
+        covers = [mask(bounds_ref, exp, unit + step) for step in (-1, 0, 1)]
+        matrices(index_ref, exp, covers, taps_ref, row_ref, own_ref, edge_ref)
     for exp in range(exp_count):
         arrivals[3 + exp].wait()
         fill_window(window_ref, exp, pixels_ref[exp].astype(jnp.float32))
@@ -145,9 +146,9 @@
 
 
 def strip_sums(
-    bounds_hbm, core_ref, link_ref, variance_hbm, strips_hbm, row_hbm, edge_hbm,
+    core_ref, link_ref, variance_hbm, strips_hbm, row_hbm, edge_hbm,
     keep_ref, give_ref,
-    bounds_ref, top_ref, bottom_ref, strips_ref, row_ref, edge_ref,
+    top_ref, bottom_ref, strips_ref, row_ref, edge_ref,
     window_ref, across_ref, in_sems,
 ):
     unit = lax.axis_index("patch")
@@ -159,7 +160,6 @@
     wait_all(
         start_all(
             [
-                (bounds_hbm, bounds_ref),
                 (row_hbm, row_ref),
                 (edge_hbm, edge_ref),
                 (strips_hbm, strips_ref),
@@ -172,8 +172,8 @@
     total = strips_ref[...]
     for exp in range(exp_count):
         core, link = core_ref[exp].astype(jnp.float32), link_ref[exp].astype(jnp.float32)
-        above = jnp.where(odd, core, link) * mask(bounds_ref, exp, unit - 1)
-        below = jnp.where(odd, link, core) * mask(bounds_ref, exp, unit + 1)
+        above = jnp.where(odd, core, link)
+        below = jnp.where(odd, link, core)
         fill_window(window_ref, exp, jnp.concatenate([above, below], axis=0))
         blocks = width // LANES
         filtered = row_filter(window_ref, exp, row_ref[exp], 0, blocks)
@@ -188,7 +188,7 @@
             edge_ref[exp, :, : 2 * NCOMP * EDGE], across_ref[exp], preferred_element_type=jnp.float32
         )
         weights = jnp.concatenate([top_ref[exp], bottom_ref[exp]], axis=0).astype(jnp.float32)
-        total = total + weights * mask(bounds_ref, exp, unit) * smoothed
+        total = total + weights * smoothed
     for x in range(near):
         first = total[:, x * share : (x + 1) * share]
         second = total[:, (near + x) * share : (near + x + 1) * share]
@@ -253,21 +253,20 @@
     strip_keep, strip_give = pl.pallas_call(
         strip_sums,
         out_shape=(keep_shape, give_shape),
-        in_specs=[hbm, vmem_spec, vmem_spec, hbm, hbm, hbm, hbm],
+        in_specs=[vmem_spec, vmem_spec, hbm, hbm, hbm, hbm],
         out_specs=(vmem_spec,) * 2,
         scratch_shapes=[
-            pltpu.SMEM(strip_bounds.shape, jnp.int32),
             *[vmem(strip)] * 2,
             vmem(edge_rows),
             vmem(row_mat),
             vmem(edge_mat),
             pltpu.VMEM((exp_count, 2 * EDGE, width + LANES), bf16),
             pltpu.VMEM((exp_count, 2 * NCOMP * EDGE, width), bf16),
-            pltpu.SemaphoreType.DMA((6,)),
+            pltpu.SemaphoreType.DMA((5,)),
         ],
         compiler_params=pltpu.CompilerParams(vmem_limit_bytes=12 * 1024 * 1024),
         name="strip_sums",
-    )(strip_bounds, from_core, from_link, inv_variance, strips, row_mats, edge_mats)
+    )(from_core, from_link, inv_variance, strips, row_mats, edge_mats)
     received, strip_give = lax.optimization_barrier((received, strip_give))
     received = received.reshape(near, FAR, lines, share)
 

time: 46.2 us -> 45.2 us (0.978)
  waiting for transfers between devices: 10.2 us -> 9.09 us
  starting transfers between devices: 27.3 us -> 28.4 us
  local copies, waits for them, and re-layouts: 0.7 us -> 0.04 us
    ppermute x1, waiting for transfers between devices: 1.08 us -> 0.01 us  [shards(): lax.ppermute(strip_give, 'epoch', swap).astype(f32)]
    all_to_all x1, starting transfers between devices: 3.73 us -> 4.81 us  [shards(): lax.all_to_all(strip_sum, 'epoch', 0, 0, tiled=True, axis_index_groups=gr...]
    ppermute x1, starting transfers between devices: 3.98 us -> 4.96 us  [shards(): lax.ppermute(strip_give, 'epoch', swap).astype(f32)]
    ppermute x1, starting transfers between devices: 5.21 us -> 4.23 us  [shards(): inner = keep + lax.ppermute(give, 'epoch', swap).astype(f32)]
    all_to_all x1, waiting for transfers between devices: 4.52 us -> 3.66 us  [shards(): lax.all_to_all(strip_sum, 'epoch', 0, 0, tiled=True, axis_index_groups=gr...]
    ppermute x1, waiting for transfers between devices: 0.01 us -> 0.77 us  [shards(): inner = keep + lax.ppermute(give, 'epoch', swap).astype(f32)]
    unnamed x12 -> x10, local copies, waits for them, and re-layouts: 0.68 us -> 0.03 us
where the time goes in v5:
time: 45.2 us; the launch traced here: 44.8 us
  starting transfers between devices  28.4 us (63%)
  waiting for transfers between devices  9.09 us (20%)
  Pallas kernels  4.98 us (11%)
  other arithmetic  1.52 us (3%)
  between operations  0.81 us (2%)
    ppermute x1, starting transfers between devices, shards(): lax.ppermute(to_core, 'patch', [(at, at ^ 1) for at in range(patches)])  7.46 us
    all_to_all x1, starting transfers between devices, shards(): lax.all_to_all(sums, 'epoch', 0, 0, tiled=True, axis_index_groups=groups)  4.99 us
    ppermute x1, starting transfers between devices, shards(): lax.ppermute(strip_give, 'epoch', swap).astype(f32)  4.96 us
    all_to_all x1, starting transfers between devices, shards(): lax.all_to_all(strip_sum, 'epoch', 0, 0, tiled=True, axis_index_groups=gr...  4.81 us
    ppermute x1, waiting for transfers between devices, shards(): lax.ppermute(to_link, 'patch', [(at, (at + 1 ^ 1) - 1) for at in range(1,...  4.64 us
    ppermute x1, starting transfers between devices, shards(): inner = keep + lax.ppermute(give, 'epoch', swap).astype(f32)  4.23 us
    pallas_call x1, Pallas kernels, shards(): pl.pallas_call(own_sums, out_shape=(sends, strip, strip, edge_rows, row_m...  3.82 us
    all_to_all x1, waiting for transfers between devices, shards(): lax.all_to_all(strip_sum, 'epoch', 0, 0, tiled=True, axis_index_groups=gr...  3.66 us
  transfers between devices with their start and end apart: 6, of which 3 were waited for; matrix products, arithmetic and copies ran while one was open for 2% of the time, Pallas kernels for 3%

profile of v5, /device:TPU:1, one launch (start us, length us, event | category | flops | bytes accessed | tf_op | source)
XLA Modules:
  0.0 44.8 jit_solution(2045484907183074949)
XLA Ops:
  0.6 3.8 %own_sums.1 = (bf16[4,448,256]{2,1,0:T(8,128)(2,1)}, bf16[2,16,2048]{2,1,0:T(8,128)(2,1)}, bf16[2,16,2048]{2,1,0:T(8,128)(2,1)}, f32[32,2048]{1,0:T(8,128)}, bf1...) custom-call(s32[2,2,2]{2,1,0:T(2,128)} %index_hbm.1, s32[2,2]{1,0:T(2,128)} %bounds_hbm.1, f32[16,21]{1,0:T(8,128)} %bank_hbm.1, ...), custom_call_target="tpu_custom_call" | custom-call | tf_op jit(solution)/shard_map/own_sums/pallas_call | solution.py:222
  4.5 0.0 copy-start
  4.5 0.0 copy-start.4
  4.5 0.0 copy-start.1
  4.5 0.0 copy-start.2
  4.5 0.0 copy-start.3
  4.5 5.0 %all-to-all-start = ((bf16[4,448,256]{2,1,0:T(8,128)(2,1)}), bf16[4,448,256]{2,1,0:T(8,128)(2,1)S(1)}, u32[]{:S(2)}, u32[]{:S(2)}) async-start(bf16[4,448,256]{2,1,0:T(8,128)(2,1)} %get-tuple-element.18), calls=%async_computation | async-start | bytes 1835008 | tf_op jit(solution)/shard_map/all_to_all | solution.py:247
  9.5 7.5 %collective-permute-start = (bf16[2,16,2048]{2,1,0:T(8,128)(2,1)}, bf16[2,16,2048]{2,1,0:T(8,128)(2,1)S(1)}, u32[]{:S(2)}, u32[]{:S(2)}) collective-permute-start(bf16[2,16,2048]{2,1,0:T(8,128)(2,1)} %get-tuple-element.12), channel_id=1, source_target_pairs={{0,32},{32,0},{64,96},{96,64},{128,160},{160,128},{192,224},{224,1... | collective-permute-start | bytes 393224 | tf_op jit(solution)/shard_map/ppermute | solution.py:249
  17.0 1.9 %collective-permute-start.1 = (bf16[2,16,2048]{2,1,0:T(8,128)(2,1)S(1)}, bf16[2,16,2048]{2,1,0:T(8,128)(2,1)S(1)}, u32[]{:S(2)}, u32[]{:S(2)}) collective-permute-start(bf16[2,16,2048]{2,1,0:T(8,128)(2,1)S(1)} %copy-done.4), channel_id=1, source_target_pairs={{32,64},{64,32},{96,128},{128,96},{160,192},{192,160},{224,256},{2... | collective-permute-start | bytes 393224 | tf_op jit(solution)/shard_map/ppermute | solution.py:250
  18.9 0.0 collective-permute-done.core_ref
  18.9 4.6 %collective-permute-done.1.link_ref = bf16[2,16,2048]{2,1,0:T(8,128)(2,1)S(1)} collective-permute-done((bf16[2,16,2048]{2,1,0:T(8,128)(2,1)S(1)}, bf16[2,16,2048]{2,1,0:T(8,128)(2,1)S(1)}, u32[]{:S(2)}, u32[]{:S(2)}) %collective-permute-start.1) | collective-permute-done | bytes 131104 | tf_op jit(solution)/shard_map/ppermute | solution.py:250
  23.6 0.0 copy-done.2
  23.6 1.2 %strip_sums.1 = (f32[4,32,256]{2,1,0:T(8,128)S(1)}, bf16[4,32,256]{2,1,0:T(8,128)(2,1)S(1)}) custom-call(bf16[2,16,2048]{2,1,0:T(8,128)(2,1)S(1)} %collective-permute-done.core_ref, bf16[2,16,2048]{2,1,0:T(8,128)(2,1)S(1)} %collective-permute-done.1.link_ref, bf16[2,128,2048]{2,1,0:T(8,128)(2,1)S(1)} %copy-done, f32[32,2048]{1,0:T(8,128)S(1)} %copy-done.1, ...), custom_call_target="tpu_custom_call" | custom-call | tf_op jit(solution)/shard_map/strip_sums/pallas_call | solution.py:253
  24.7 0.0 all-to-all-done
  24.8 5.0 %collective-permute-start.2 = (bf16[4,32,256]{2,1,0:T(8,128)(2,1)S(1)}, bf16[4,32,256]{2,1,0:T(8,128)(2,1)S(1)}, u32[]{:S(2)}, u32[]{:S(2)}) collective-permute-start(bf16[4,32,256]{2,1,0:T(8,128)(2,1)S(1)} %get-tuple-element.20), channel_id=1, source_target_pairs={{0,16},{4,20},{8,24},{12,28},{16,0},{20,4},{24,8},{28,12},{1,17},{... | collective-permute-start | bytes 196616 | tf_op jit(solution)/shard_map/ppermute | solution.py:278
  29.7 0.1 dynamic-slice_reduce_fusion
  29.8 4.2 %collective-permute-start.3 = (bf16[224,256]{1,0:T(8,128)(2,1)S(1)}, bf16[224,256]{1,0:T(8,128)(2,1)S(1)}, u32[]{:S(2)}, u32[]{:S(2)}) collective-permute-start(bf16[224,256]{1,0:T(8,128)(2,1)S(1)} %dynamic-slice_reduce_fusion), channel_id=1, source_target_pairs={{0,16},{4,20},{8,24},{12,28},{16,0},{20,4},{24,8},{28,12},{1,17},{... | collective-permute-start | bytes 344072 | tf_op jit(solution)/shard_map/ppermute | solution.py:277
  34.0 0.1 convert_reduce_fusion
  34.1 0.0 collective-permute-done.2
  34.1 0.6 %add_convert_fusion = bf16[4,32,256]{2,1,0:T(8,128)(2,1)} fusion(f32[4,32,256]{2,1,0:T(8,128)S(1)} %get-tuple-element.17, bf16[4,32,256]{2,1,0:T(8,128)(2,1)S(1)} %collective-permute-done.2), kind=kLoop, calls=%fused_computation.5 | loop fusion | flops 98304 | bytes 262144 | tf_op jit(solution)/shard_map/convert_element_type | solution.py:278
  34.8 4.8 %all-to-all-start.1 = ((bf16[4,32,256]{2,1,0:T(8,128)(2,1)}), bf16[4,32,256]{2,1,0:T(8,128)(2,1)S(1)}, u32[]{:S(2)}, u32[]{:S(2)}) async-start(bf16[4,32,256]{2,1,0:T(8,128)(2,1)} %add_convert_fusion), calls=%async_computation.1 | async-start | bytes 131072 | tf_op jit(solution)/shard_map/all_to_all | solution.py:280
  39.6 0.8 %collective-permute-done.3 = bf16[224,256]{1,0:T(8,128)(2,1)S(1)} collective-permute-done((bf16[224,256]{1,0:T(8,128)(2,1)S(1)}, bf16[224,256]{1,0:T(8,128)(2,1)S(1)}, u32[]{:S(2)}, u32[]{:S(2)}) %collective-permute-start.3) | collective-permute-done | bytes 114720 | tf_op jit(solution)/shard_map/ppermute | solution.py:277
  40.4 3.7 %all-to-all-done.1 = bf16[4,32,256]{2,1,0:T(8,128)(2,1)S(1)} async-done(((bf16[4,32,256]{2,1,0:T(8,128)(2,1)}), bf16[4,32,256]{2,1,0:T(8,128)(2,1)S(1)}, u32[]{:S(2)}, u32[]{:S(2)}) %all-to-all-start.1) | async-done | bytes 65568 | tf_op jit(solution)/shard_map/all_to_all | solution.py:280
  44.1 0.7 %maximum_divide_fusion = (f32[128,256]{1,0:T(8,128)}, f32[128,256]{1,0:T(8,128)}) fusion(f32[16,256]{1,0:T(8,128)S(1)} %get-tuple-element.25, f32[96,256]{1,0:T(8,128)S(1)} %slice.17, f32[16,256]{1,0:T(8,128)S(1)} %get-tuple-element.24, f32[224,256]{1,0:T(8,128)S(1)} %convert_add_fusion), kind=kLoop, calls=%fused_computation.3 | loop fusion | flops 131072 | bytes 524288 | tf_op jit(solution)/shard_map/div | solution.py:285
  (8 shorter events, 0.1 us)
Async XLA Ops:
  4.5 19.1 %copy-start = (bf16[2,128,2048]{2,1,0:T(8,128)(2,1)S(1)}, bf16[2,128,2048]{2,1,0:T(8,128)(2,1)}, u32[]{:S(2)}) copy-start(bf16[2,128,2048]{2,1,0:T(8,128)(2,1)} %variance_hbm.3) | copy-start | bytes 3145732
  4.5 12.5 %copy-start.4 = (bf16[2,16,2048]{2,1,0:T(8,128)(2,1)S(1)}, bf16[2,16,2048]{2,1,0:T(8,128)(2,1)}, u32[]{:S(2)}) copy-start(bf16[2,16,2048]{2,1,0:T(8,128)(2,1)} %get-tuple-element.13) | copy-start | bytes 393220
  4.5 19.1 %copy-start.1 = (f32[32,2048]{1,0:T(8,128)S(1)}, f32[32,2048]{1,0:T(8,128)}, u32[]{:S(2)}) copy-start(f32[32,2048]{1,0:T(8,128)} %get-tuple-element.14.strips_hbm) | copy-start | bytes 786436
  4.5 19.1 %copy-start.2 = (bf16[2,256,256]{2,1,0:T(8,128)(2,1)S(1)}, bf16[2,256,256]{2,1,0:T(8,128)(2,1)}, u32[]{:S(2)}) copy-start(bf16[2,256,256]{2,1,0:T(8,128)(2,1)} %get-tuple-element.15.row_hbm) | copy-start | bytes 786436
  4.5 19.1 %copy-start.3 = (bf16[2,32,128]{2,1,0:T(8,128)(2,1)S(1)}, bf16[2,32,128]{2,1,0:T(8,128)(2,1)}, u32[]{:S(2)}) copy-start(bf16[2,32,128]{2,1,0:T(8,128)(2,1)} %get-tuple-element.16.edge_hbm) | copy-start | bytes 49156
  4.5 20.2 %all-to-all-start = ((bf16[4,448,256]{2,1,0:T(8,128)(2,1)}), bf16[4,448,256]{2,1,0:T(8,128)(2,1)S(1)}, u32[]{:S(2)}, u32[]{:S(2)}) async-start(bf16[4,448,256]{2,1,0:T(8,128)(2,1)} %get-tuple-element.18), calls=%async_computation | async-start | bytes 1835008 | tf_op jit(solution)/shard_map/all_to_all | solution.py:247
  9.5 9.4 %collective-permute-start = (bf16[2,16,2048]{2,1,0:T(8,128)(2,1)}, bf16[2,16,2048]{2,1,0:T(8,128)(2,1)S(1)}, u32[]{:S(2)}, u32[]{:S(2)}) collective-permute-start(bf16[2,16,2048]{2,1,0:T(8,128)(2,1)} %get-tuple-element.12), channel_id=1, source_target_pairs={{0,32},{32,0},{64,96},{96,64},{128,160},{160,128},{192,224},{224,1... | collective-permute-start | bytes 393224 | tf_op jit(solution)/shard_map/ppermute | solution.py:249
  17.0 6.6 %collective-permute-start.1 = (bf16[2,16,2048]{2,1,0:T(8,128)(2,1)S(1)}, bf16[2,16,2048]{2,1,0:T(8,128)(2,1)S(1)}, u32[]{:S(2)}, u32[]{:S(2)}) collective-permute-start(bf16[2,16,2048]{2,1,0:T(8,128)(2,1)S(1)} %copy-done.4), channel_id=1, source_target_pairs={{32,64},{64,32},{96,128},{128,96},{160,192},{192,160},{224,256},{2... | collective-permute-start | bytes 393224 | tf_op jit(solution)/shard_map/ppermute | solution.py:250
  24.8 9.4 %collective-permute-start.2 = (bf16[4,32,256]{2,1,0:T(8,128)(2,1)S(1)}, bf16[4,32,256]{2,1,0:T(8,128)(2,1)S(1)}, u32[]{:S(2)}, u32[]{:S(2)}) collective-permute-start(bf16[4,32,256]{2,1,0:T(8,128)(2,1)S(1)} %get-tuple-element.20), channel_id=1, source_target_pairs={{0,16},{4,20},{8,24},{12,28},{16,0},{20,4},{24,8},{28,12},{1,17},{... | collective-permute-start | bytes 196616 | tf_op jit(solution)/shard_map/ppermute | solution.py:278
  29.8 10.5 %collective-permute-start.3 = (bf16[224,256]{1,0:T(8,128)(2,1)S(1)}, bf16[224,256]{1,0:T(8,128)(2,1)S(1)}, u32[]{:S(2)}, u32[]{:S(2)}) collective-permute-start(bf16[224,256]{1,0:T(8,128)(2,1)S(1)} %dynamic-slice_reduce_fusion), channel_id=1, source_target_pairs={{0,16},{4,20},{8,24},{12,28},{16,0},{20,4},{24,8},{28,12},{1,17},{... | collective-permute-start | bytes 344072 | tf_op jit(solution)/shard_map/ppermute | solution.py:277
  34.8 9.3 %all-to-all-start.1 = ((bf16[4,32,256]{2,1,0:T(8,128)(2,1)}), bf16[4,32,256]{2,1,0:T(8,128)(2,1)S(1)}, u32[]{:S(2)}, u32[]{:S(2)}) async-start(bf16[4,32,256]{2,1,0:T(8,128)(2,1)} %add_convert_fusion), calls=%async_computation.1 | async-start | bytes 131072 | tf_op jit(solution)/shard_map/all_to_all | solution.py:280

commit v6 on v5

--- a/solution.py
+++ b/solution.py
@@ -99,17 +99,7 @@
     for exp in range(exp_count):
         covers = [mask(bounds_ref, exp, unit + step) for step in (-1, 0, 1)]
         matrices(index_ref, exp, covers, taps_ref, row_ref, own_ref, edge_ref)
-    for exp in range(exp_count):
-        arrivals[3 + exp].wait()
-        fill_window(window_ref, exp, pixels_ref[exp].astype(jnp.float32))
-        for start in range(0, width // LANES, GROUP):
-            filtered = row_filter(window_ref, exp, row_ref[exp], start, GROUP)
-            for block in range(GROUP):
-                at = slice((start + block) * LANES, (start + block + 1) * LANES)
-                for comp in range(NCOMP):
-                    across_ref[exp, comp * UNIT : (comp + 1) * UNIT, at] = filtered[
-                        block * UNIT : (block + 1) * UNIT, comp * LANES : (comp + 1) * LANES
-                    ]
+    wait_all(arrivals[3 : 3 + exp_count])
     to_core = pl.multiple_of((1 - odd) * (rows - EDGE), EDGE)
     to_link = pl.multiple_of(odd * (rows - EDGE), EDGE)
     leaves = start_all(
@@ -121,6 +111,16 @@
         ],
         out_sems,
     )
+    for exp in range(exp_count):
+        fill_window(window_ref, exp, pixels_ref[exp].astype(jnp.float32))
+        for start in range(0, width // LANES, GROUP):
+            filtered = row_filter(window_ref, exp, row_ref[exp], start, GROUP)
+            for block in range(GROUP):
+                at = slice((start + block) * LANES, (start + block + 1) * LANES)
+                for comp in range(NCOMP):
+                    across_ref[exp, comp * UNIT : (comp + 1) * UNIT, at] = filtered[
+                        block * UNIT : (block + 1) * UNIT, comp * LANES : (comp + 1) * LANES
+                    ]
     wait_all(arrivals[3 + exp_count :])
     masks = [mask(bounds_ref, exp, unit) for exp in range(exp_count)]
     for part in range(width // share):

time: 45.2 us -> 45 us (level)
  no operation moved by 1% of the time
where the time goes in v6:
time: 45 us; the launch traced here: 44.6 us
  starting transfers between devices  28.4 us (63%)
  waiting for transfers between devices  9.09 us (20%)
  Pallas kernels  4.75 us (11%)
  other arithmetic  1.52 us (3%)
  between operations  0.81 us (2%)
    ppermute x1, starting transfers between devices, shards(): lax.ppermute(to_core, 'patch', [(at, at ^ 1) for at in range(patches)])  7.46 us
    all_to_all x1, starting transfers between devices, shards(): lax.all_to_all(sums, 'epoch', 0, 0, tiled=True, axis_index_groups=groups)  4.99 us
    ppermute x1, starting transfers between devices, shards(): lax.ppermute(strip_give, 'epoch', swap).astype(f32)  4.97 us
    all_to_all x1, starting transfers between devices, shards(): lax.all_to_all(strip_sum, 'epoch', 0, 0, tiled=True, axis_index_groups=gr...  4.81 us
    ppermute x1, waiting for transfers between devices, shards(): lax.ppermute(to_link, 'patch', [(at, (at + 1 ^ 1) - 1) for at in range(1,...  4.64 us
    ppermute x1, starting transfers between devices, shards(): inner = keep + lax.ppermute(give, 'epoch', swap).astype(f32)  4.22 us
    all_to_all x1, waiting for transfers between devices, shards(): lax.all_to_all(strip_sum, 'epoch', 0, 0, tiled=True, axis_index_groups=gr...  3.65 us
    pallas_call x1, Pallas kernels, shards(): pl.pallas_call(own_sums, out_shape=(sends, strip, strip, edge_rows, row_m...  3.58 us
  transfers between devices with their start and end apart: 6, of which 3 were waited for; matrix products, arithmetic and copies ran while one was open for 2% of the time, Pallas kernels for 3%

profile of v6, /device:TPU:1, one launch (start us, length us, event | category | flops | bytes accessed | tf_op | source)
XLA Modules:
  0.0 44.6 jit_solution(3069179116003625738)
XLA Ops:
  0.6 3.6 %own_sums.1 = (bf16[4,448,256]{2,1,0:T(8,128)(2,1)}, bf16[2,16,2048]{2,1,0:T(8,128)(2,1)}, bf16[2,16,2048]{2,1,0:T(8,128)(2,1)}, f32[32,2048]{1,0:T(8,128)}, bf1...) custom-call(s32[2,2,2]{2,1,0:T(2,128)} %index_hbm.1, s32[2,2]{1,0:T(2,128)} %bounds_hbm.1, f32[16,21]{1,0:T(8,128)} %bank_hbm.1, ...), custom_call_target="tpu_custom_call" | custom-call | tf_op jit(solution)/shard_map/own_sums/pallas_call | solution.py:222
  4.2 0.0 copy-start
  4.2 0.0 copy-start.4
  4.2 0.0 copy-start.1
  4.3 0.0 copy-start.2
  4.3 0.0 copy-start.3
  4.3 5.0 %all-to-all-start = ((bf16[4,448,256]{2,1,0:T(8,128)(2,1)}), bf16[4,448,256]{2,1,0:T(8,128)(2,1)S(1)}, u32[]{:S(2)}, u32[]{:S(2)}) async-start(bf16[4,448,256]{2,1,0:T(8,128)(2,1)} %get-tuple-element.18), calls=%async_computation | async-start | bytes 1835008 | tf_op jit(solution)/shard_map/all_to_all | solution.py:247
  9.3 7.5 %collective-permute-start = (bf16[2,16,2048]{2,1,0:T(8,128)(2,1)}, bf16[2,16,2048]{2,1,0:T(8,128)(2,1)S(1)}, u32[]{:S(2)}, u32[]{:S(2)}) collective-permute-start(bf16[2,16,2048]{2,1,0:T(8,128)(2,1)} %get-tuple-element.12), channel_id=1, source_target_pairs={{0,32},{32,0},{64,96},{96,64},{128,160},{160,128},{192,224},{224,1... | collective-permute-start | bytes 393224 | tf_op jit(solution)/shard_map/ppermute | solution.py:249
  16.7 0.0 copy-done.4
  16.7 1.9 %collective-permute-start.1 = (bf16[2,16,2048]{2,1,0:T(8,128)(2,1)S(1)}, bf16[2,16,2048]{2,1,0:T(8,128)(2,1)S(1)}, u32[]{:S(2)}, u32[]{:S(2)}) collective-permute-start(bf16[2,16,2048]{2,1,0:T(8,128)(2,1)S(1)} %copy-done.4), channel_id=1, source_target_pairs={{32,64},{64,32},{96,128},{128,96},{160,192},{192,160},{224,256},{2... | collective-permute-start | bytes 393224 | tf_op jit(solution)/shard_map/ppermute | solution.py:250
  18.7 0.0 collective-permute-done.core_ref
  18.7 4.6 %collective-permute-done.1.link_ref = bf16[2,16,2048]{2,1,0:T(8,128)(2,1)S(1)} collective-permute-done((bf16[2,16,2048]{2,1,0:T(8,128)(2,1)S(1)}, bf16[2,16,2048]{2,1,0:T(8,128)(2,1)S(1)}, u32[]{:S(2)}, u32[]{:S(2)}) %collective-permute-start.1) | collective-permute-done | bytes 131104 | tf_op jit(solution)/shard_map/ppermute | solution.py:250
  23.3 1.2 %strip_sums.1 = (f32[4,32,256]{2,1,0:T(8,128)S(1)}, bf16[4,32,256]{2,1,0:T(8,128)(2,1)S(1)}) custom-call(bf16[2,16,2048]{2,1,0:T(8,128)(2,1)S(1)} %collective-permute-done.core_ref, bf16[2,16,2048]{2,1,0:T(8,128)(2,1)S(1)} %collective-permute-done.1.link_ref, bf16[2,128,2048]{2,1,0:T(8,128)(2,1)S(1)} %copy-done, f32[32,2048]{1,0:T(8,128)S(1)} %copy-done.1, ...), custom_call_target="tpu_custom_call" | custom-call | tf_op jit(solution)/shard_map/strip_sums/pallas_call | solution.py:253
  24.5 0.0 all-to-all-done
  24.5 5.0 %collective-permute-start.2 = (bf16[4,32,256]{2,1,0:T(8,128)(2,1)S(1)}, bf16[4,32,256]{2,1,0:T(8,128)(2,1)S(1)}, u32[]{:S(2)}, u32[]{:S(2)}) collective-permute-start(bf16[4,32,256]{2,1,0:T(8,128)(2,1)S(1)} %get-tuple-element.20), channel_id=1, source_target_pairs={{0,16},{4,20},{8,24},{12,28},{16,0},{20,4},{24,8},{28,12},{1,17},{... | collective-permute-start | bytes 196616 | tf_op jit(solution)/shard_map/ppermute | solution.py:278
  29.5 0.1 dynamic-slice_reduce_fusion
  29.6 4.2 %collective-permute-start.3 = (bf16[224,256]{1,0:T(8,128)(2,1)S(1)}, bf16[224,256]{1,0:T(8,128)(2,1)S(1)}, u32[]{:S(2)}, u32[]{:S(2)}) collective-permute-start(bf16[224,256]{1,0:T(8,128)(2,1)S(1)} %dynamic-slice_reduce_fusion), channel_id=1, source_target_pairs={{0,16},{4,20},{8,24},{12,28},{16,0},{20,4},{24,8},{28,12},{1,17},{... | collective-permute-start | bytes 344072 | tf_op jit(solution)/shard_map/ppermute | solution.py:277
  33.8 0.1 convert_reduce_fusion
  33.9 0.0 collective-permute-done.2
  33.9 0.6 %add_convert_fusion = bf16[4,32,256]{2,1,0:T(8,128)(2,1)} fusion(f32[4,32,256]{2,1,0:T(8,128)S(1)} %get-tuple-element.17, bf16[4,32,256]{2,1,0:T(8,128)(2,1)S(1)} %collective-permute-done.2), kind=kLoop, calls=%fused_computation.5 | loop fusion | flops 98304 | bytes 262144 | tf_op jit(solution)/shard_map/convert_element_type | solution.py:278
  34.5 4.8 %all-to-all-start.1 = ((bf16[4,32,256]{2,1,0:T(8,128)(2,1)}), bf16[4,32,256]{2,1,0:T(8,128)(2,1)S(1)}, u32[]{:S(2)}, u32[]{:S(2)}) async-start(bf16[4,32,256]{2,1,0:T(8,128)(2,1)} %add_convert_fusion), calls=%async_computation.1 | async-start | bytes 131072 | tf_op jit(solution)/shard_map/all_to_all | solution.py:280
  39.3 0.8 %collective-permute-done.3 = bf16[224,256]{1,0:T(8,128)(2,1)S(1)} collective-permute-done((bf16[224,256]{1,0:T(8,128)(2,1)S(1)}, bf16[224,256]{1,0:T(8,128)(2,1)S(1)}, u32[]{:S(2)}, u32[]{:S(2)}) %collective-permute-start.3) | collective-permute-done | bytes 114720 | tf_op jit(solution)/shard_map/ppermute | solution.py:277
  40.2 3.7 %all-to-all-done.1 = bf16[4,32,256]{2,1,0:T(8,128)(2,1)S(1)} async-done(((bf16[4,32,256]{2,1,0:T(8,128)(2,1)}), bf16[4,32,256]{2,1,0:T(8,128)(2,1)S(1)}, u32[]{:S(2)}, u32[]{:S(2)}) %all-to-all-start.1) | async-done | bytes 65568 | tf_op jit(solution)/shard_map/all_to_all | solution.py:280
  43.9 0.7 %maximum_divide_fusion = (f32[128,256]{1,0:T(8,128)}, f32[128,256]{1,0:T(8,128)}) fusion(f32[16,256]{1,0:T(8,128)S(1)} %get-tuple-element.25, f32[96,256]{1,0:T(8,128)S(1)} %slice.17, f32[16,256]{1,0:T(8,128)S(1)} %get-tuple-element.24, f32[224,256]{1,0:T(8,128)S(1)} %convert_add_fusion), kind=kLoop, calls=%fused_computation.3 | loop fusion | flops 131072 | bytes 524288 | tf_op jit(solution)/shard_map/div | solution.py:285
  (8 shorter events, 0.1 us)
Async XLA Ops:
  4.2 19.1 %copy-start = (bf16[2,128,2048]{2,1,0:T(8,128)(2,1)S(1)}, bf16[2,128,2048]{2,1,0:T(8,128)(2,1)}, u32[]{:S(2)}) copy-start(bf16[2,128,2048]{2,1,0:T(8,128)(2,1)} %variance_hbm.3) | copy-start | bytes 3145732
  4.2 12.5 %copy-start.4 = (bf16[2,16,2048]{2,1,0:T(8,128)(2,1)S(1)}, bf16[2,16,2048]{2,1,0:T(8,128)(2,1)}, u32[]{:S(2)}) copy-start(bf16[2,16,2048]{2,1,0:T(8,128)(2,1)} %get-tuple-element.13) | copy-start | bytes 393220
  4.2 19.1 %copy-start.1 = (f32[32,2048]{1,0:T(8,128)S(1)}, f32[32,2048]{1,0:T(8,128)}, u32[]{:S(2)}) copy-start(f32[32,2048]{1,0:T(8,128)} %get-tuple-element.14.strips_hbm) | copy-start | bytes 786436
  4.3 19.1 %copy-start.2 = (bf16[2,256,256]{2,1,0:T(8,128)(2,1)S(1)}, bf16[2,256,256]{2,1,0:T(8,128)(2,1)}, u32[]{:S(2)}) copy-start(bf16[2,256,256]{2,1,0:T(8,128)(2,1)} %get-tuple-element.15.row_hbm) | copy-start | bytes 786436
  4.3 19.1 %copy-start.3 = (bf16[2,32,128]{2,1,0:T(8,128)(2,1)S(1)}, bf16[2,32,128]{2,1,0:T(8,128)(2,1)}, u32[]{:S(2)}) copy-start(bf16[2,32,128]{2,1,0:T(8,128)(2,1)} %get-tuple-element.16.edge_hbm) | copy-start | bytes 49156
  4.3 20.2 %all-to-all-start = ((bf16[4,448,256]{2,1,0:T(8,128)(2,1)}), bf16[4,448,256]{2,1,0:T(8,128)(2,1)S(1)}, u32[]{:S(2)}, u32[]{:S(2)}) async-start(bf16[4,448,256]{2,1,0:T(8,128)(2,1)} %get-tuple-element.18), calls=%async_computation | async-start | bytes 1835008 | tf_op jit(solution)/shard_map/all_to_all | solution.py:247
  9.3 9.4 %collective-permute-start = (bf16[2,16,2048]{2,1,0:T(8,128)(2,1)}, bf16[2,16,2048]{2,1,0:T(8,128)(2,1)S(1)}, u32[]{:S(2)}, u32[]{:S(2)}) collective-permute-start(bf16[2,16,2048]{2,1,0:T(8,128)(2,1)} %get-tuple-element.12), channel_id=1, source_target_pairs={{0,32},{32,0},{64,96},{96,64},{128,160},{160,128},{192,224},{224,1... | collective-permute-start | bytes 393224 | tf_op jit(solution)/shard_map/ppermute | solution.py:249
  16.7 6.6 %collective-permute-start.1 = (bf16[2,16,2048]{2,1,0:T(8,128)(2,1)S(1)}, bf16[2,16,2048]{2,1,0:T(8,128)(2,1)S(1)}, u32[]{:S(2)}, u32[]{:S(2)}) collective-permute-start(bf16[2,16,2048]{2,1,0:T(8,128)(2,1)S(1)} %copy-done.4), channel_id=1, source_target_pairs={{32,64},{64,32},{96,128},{128,96},{160,192},{192,160},{224,256},{2... | collective-permute-start | bytes 393224 | tf_op jit(solution)/shard_map/ppermute | solution.py:250
  24.5 9.4 %collective-permute-start.2 = (bf16[4,32,256]{2,1,0:T(8,128)(2,1)S(1)}, bf16[4,32,256]{2,1,0:T(8,128)(2,1)S(1)}, u32[]{:S(2)}, u32[]{:S(2)}) collective-permute-start(bf16[4,32,256]{2,1,0:T(8,128)(2,1)S(1)} %get-tuple-element.20), channel_id=1, source_target_pairs={{0,16},{4,20},{8,24},{12,28},{16,0},{20,4},{24,8},{28,12},{1,17},{... | collective-permute-start | bytes 196616 | tf_op jit(solution)/shard_map/ppermute | solution.py:278
  29.6 10.6 %collective-permute-start.3 = (bf16[224,256]{1,0:T(8,128)(2,1)S(1)}, bf16[224,256]{1,0:T(8,128)(2,1)S(1)}, u32[]{:S(2)}, u32[]{:S(2)}) collective-permute-start(bf16[224,256]{1,0:T(8,128)(2,1)S(1)} %dynamic-slice_reduce_fusion), channel_id=1, source_target_pairs={{0,16},{4,20},{8,24},{12,28},{16,0},{20,4},{24,8},{28,12},{1,17},{... | collective-permute-start | bytes 344072 | tf_op jit(solution)/shard_map/ppermute | solution.py:277
  34.5 9.3 %all-to-all-start.1 = ((bf16[4,32,256]{2,1,0:T(8,128)(2,1)}), bf16[4,32,256]{2,1,0:T(8,128)(2,1)S(1)}, u32[]{:S(2)}, u32[]{:S(2)}) async-start(bf16[4,32,256]{2,1,0:T(8,128)(2,1)} %add_convert_fusion), calls=%async_computation.1 | async-start | bytes 131072 | tf_op jit(solution)/shard_map/all_to_all | solution.py:280
